TPU v7x, 32 devices: a whole 2x2x4 slice. The times are simulated.
32 devices in a mesh: req: 8 (over z, y), tp: 4 (over x, core).
Axes of the slice: x: 2, y: 2, z: 4, core: 2. Of those that a mesh axis runs over, the one named last changes fastest.
Arguments:
- tokens: bfloat16 [4096, 4096], P('req', 'tp'), may hold values from -400 to 400
- input_norm_gain: float32 [4096], replicated, may hold values from 0.1 to 1.9
- query_weight: bfloat16 [4096, 2048], P(None, 'tp'), may hold values from -0.078125 to 0.078125
- key_weight: bfloat16 [4096, 2048], P(None, 'tp'), may hold values from -1.953125 to 1.953125
- value_weight: bfloat16 [4096, 2048], P(None, 'tp'), may hold values from -0.09375 to 0.09375
- query_down_maps: bfloat16 [4096, 512], replicated, may hold values from -0.09375 to 0.09375
- value_down_maps: bfloat16 [4096, 512], replicated, may hold values from -0.09375 to 0.09375
- query_up_maps: bfloat16 [512, 2048], P(None, 'tp'), may hold values from -1.5 to 1.5
- value_up_maps: bfloat16 [512, 2048], P(None, 'tp'), may hold values from -1.5 to 1.5
- lengths: int32 [4], replicated, may hold values from 1 to 2304, 4096 in all
- prompt_adapter_index: int32 [4], replicated, may hold values from 0 to 31
Outputs:
- attended: bfloat16 [4096, 2048], P('req', 'tp')
Inputs may be any that keep to these rules, and one draw needn't show every extreme that they name: `lengths`: the longest prompt has exactly 2304 tokens.
All inputs are finite; a program needn't handle non-finite values.
Results may differ from a plain program's by a relative error of at most 0.0083.
Values may be sent and summed in bfloat16 or wider, within the bound.
A program may use at most 192 MiB of HBM per device.

v0:
```python
import math

import jax
import jax.numpy as jnp
from jax import lax
from jax.sharding import PartitionSpec as P

HEAD = 128
ADAPTER_RANK = 16
ADAPTER_COUNT = 32


EPS = 1e-05
ADAPTER_SCALE = 0.5
MASKED = -1e30


def prompt_layout(lengths, positions):
    ends = jnp.cumsum(lengths)
    before = (ends[None, :] <= positions[:, None]).astype(jnp.int32)
    starts = jnp.sum(before * lengths[None, :], axis=1)
    prompt = jnp.sum(before, axis=1)
    return (starts, prompt)


def adapter_mask(prompt, prompt_adapter_index, count, rank):
    chosen = (
        prompt[:, None] == jnp.arange(prompt_adapter_index.shape[0], dtype=jnp.int32)[None, :]
    ).astype(jnp.int32)
    adapter = jnp.sum(chosen * prompt_adapter_index[None, :], axis=1)
    column = jnp.arange(count * rank, dtype=jnp.int32) // rank
    return (column[None, :] == adapter[:, None]).astype(jnp.float32)


def rotate(field, offsets, width):
    half = width // 2
    freq = jnp.exp(jnp.arange(half, dtype=jnp.float32) * (-2.0 * math.log(10000.0) / width))
    angle = offsets.astype(jnp.float32)[:, None] * freq[None, :]
    cosine = jnp.cos(angle)[:, None, :]
    sine = jnp.sin(angle)[:, None, :]
    first = field[..., :half]
    second = field[..., half:]
    return jnp.concatenate(
        [first * cosine - second * sine, second * cosine + first * sine], axis=-1
    )


def body(
    tokens,
    input_norm_gain,
    query_weight,
    key_weight,
    value_weight,
    query_down_maps,
    value_down_maps,
    query_up_maps,
    value_up_maps,
    lengths,
    prompt_adapter_index,
):
    row_count = tokens.shape[0]
    req_index = lax.axis_index("req")
    positions = req_index * row_count + jnp.arange(row_count, dtype=jnp.int32)
    starts, prompt = prompt_layout(lengths, positions)
    causal_mask = adapter_mask(prompt, prompt_adapter_index, ADAPTER_COUNT, ADAPTER_RANK)
    incoming_weights = (query_weight, key_weight, value_weight, query_down_maps, value_down_maps)
    whole = lax.all_gather(tokens, "tp", axis=1, tiled=True)
    whole_float = whole.astype(jnp.float32)
    normed = (
        whole_float
        * lax.rsqrt(jnp.mean(whole_float * whole_float, axis=1, keepdims=True) + EPS)
        * input_norm_gain[None, :]
    ).astype(jnp.bfloat16)
    projected = tuple(
        (jnp.dot(normed, weight, preferred_element_type=jnp.float32) for weight in incoming_weights)
    )
    query_linear, key_lin, value_linear, query_middle, value_middle = projected
    query_middle = (query_middle * causal_mask).astype(jnp.bfloat16)
    value_middle = (value_middle * causal_mask).astype(jnp.bfloat16)
    query_linear = query_linear + ADAPTER_SCALE * jnp.dot(
        query_middle, query_up_maps, preferred_element_type=jnp.float32
    )
    value_rows = (
        value_linear
        + ADAPTER_SCALE * jnp.dot(value_middle, value_up_maps, preferred_element_type=jnp.float32)
    ).astype(jnp.bfloat16)
    head_count = query_linear.shape[1] // HEAD
    offsets = positions - starts
    queries = jnp.transpose(
        rotate(query_linear.reshape(row_count, head_count, HEAD), offsets, HEAD).astype(
            jnp.bfloat16
        ),
        (1, 0, 2),
    )
    keys = (
        rotate(key_lin.reshape(row_count, head_count, HEAD), offsets, HEAD)
        .astype(jnp.bfloat16)
        .reshape(row_count, head_count * HEAD)
    )
    key_value = jnp.stack([keys, value_rows])
    scale = 1.0 / math.sqrt(HEAD)

    def attend(state, block, key_first):
        peak, total, summed = state
        block_rows = block.shape[1]
        key_block = block[0].reshape(block_rows, head_count, HEAD)
        value_block = block[1].reshape(block_rows, head_count, HEAD)
        scores = (
            jnp.einsum("hqd,khd->hqk", queries, key_block, preferred_element_type=jnp.float32)
            * scale
        )
        key_pos = key_first + jnp.arange(block_rows, dtype=jnp.int32)
        allowed = (key_pos[None, :] >= starts[:, None]) & (key_pos[None, :] <= positions[:, None])
        scores = jnp.where(allowed[None], scores, MASKED)
        new_peak = jnp.maximum(peak, jnp.max(scores, axis=2))
        weights = jnp.where(allowed[None], jnp.exp(scores - new_peak[:, :, None]), 0.0)
        factor = jnp.exp(peak - new_peak)
        new_total = total * factor + jnp.sum(weights, axis=2)
        new_summed = summed * factor[:, :, None] + jnp.einsum(
            "hqk,khd->hqd",
            weights.astype(jnp.bfloat16),
            value_block,
            preferred_element_type=jnp.float32,
        )
        return (new_peak, new_total, new_summed)

    def visit(state, block, key_first):
        return attend(state, block, key_first)

    initial = (
        jnp.full((head_count, row_count), MASKED, jnp.float32),
        jnp.zeros((head_count, row_count), jnp.float32),
        jnp.zeros((head_count, row_count, HEAD), jnp.float32),
    )
    piece = lax.all_gather(key_value, "req", axis=1, tiled=True)
    piece_rows = piece.shape[1]
    block_rows = row_count

    def inner(turn, carry):
        block = lax.dynamic_slice_in_dim(piece, turn * block_rows, block_rows, 1)
        return visit(carry, block, turn * block_rows)

    state = lax.fori_loop(0, piece_rows // block_rows, inner, initial)
    peak, total, summed = state
    attended = (summed / total[:, :, None]).astype(jnp.bfloat16)
    return jnp.transpose(attended, (1, 0, 2)).reshape(row_count, head_count * HEAD)


def solution(mesh):
    in_specs = (
        P("req", "tp"),
        P(),
        P(None, "tp"),
        P(None, "tp"),
        P(None, "tp"),
        P(),
        P(),
        P(None, "tp"),
        P(None, "tp"),
        P(),
        P(),
    )
    out_specs = P("req", "tp")
    return jax.shard_map(body, mesh=mesh, in_specs=in_specs, out_specs=out_specs, check_vma=False)
```

profile of v0, /device:TPU:0, one launch (start us, length us, event | category | flops | bytes accessed | tf_op | source)
XLA Modules:
  0.0 278.4 jit_solution(7877876330141691670)
XLA Ops:
  9.7 1.8 multiply_cosine_fusion
  11.4 34.7 %all-gather.3.cloned.1.call-done = bf16[512,4096]{1,0:T(8,128)(2,1)} async-done(((bf16[512,1024]{1,0:T(8,128)(2,1)}), bf16[512,4096]{1,0:T(8,128)(2,1)}) %all-gather.3.cloned.1.call-update) | async-done | bytes 4194320 | tf_op jit(solution)/shard_map/all_gather | solution.py:67
  46.1 3.2 %fusion.15 = f32[512]{0:T(512)S(1)} fusion(bf16[512,4096]{1,0:T(8,128)(2,1)} %all-gather.3.cloned.1.call-done), kind=kLoop, calls=%fused_computation.24 | loop fusion | flops 6290944 | bytes 4196352 | tf_op jit(solution)/shard_map/reduce_sum | solution.py:71
  49.6 4.6 %fusion.40 = f32[512,512]{1,0:T(8,128)S(1)} fusion(bf16[4096,512]{1,0:T(8,128)(2,1)} %param.15, bf16[512,4096]{1,0:T(8,128)(2,1)S(1)} %copy-done.1, f32[4096]{0:T(1024)S(1)} %copy-done.8, f32[512]{0:T(512)S(1)} %add_rsqrt_fusion), kind=kOutput, calls=%fused_computation.74 | convolution fusion | flops 2155872256 | bytes 9455616 | tf_op jit(solution)/shard_map/dot_general | solution.py:75
  54.2 6.1 %fusion.18 = f32[512,512]{1,0:T(8,128)S(1)} fusion(f32[512,512]{1,0:T(8,128)S(1)} %fusion.40, bf16[512,512]{1,0:T(8,128)(2,1)S(1)} %copy-done, bf16[4096,512]{1,0:T(8,128)(2,1)} %param.18, s32[512]{0:T(512)S(1)} %add_select_fusion, s32[512]{0:T(512)S(1)} %select_reduce_fusion, bf16[512,4096]{1,0:T(8,128)(2,1)} %all-gather.3.cloned.1.call-done, ...), kind=kOutput, calls=%fused_computation.28 | convolution fusion | flops 2425618432 | bytes 11032576 | tf_op jit(solution)/shard_map/dot_general | solution.py:80
  60.6 5.9 %fusion.46 = f32[512,512]{0,1:T(8,128)S(1)} fusion(bf16[4096,512]{1,0:T(8,128)(2,1)} %param.16, bf16[512,4096]{1,0:T(8,128)(2,1)} %all-gather.3.cloned.1.call-done, f32[4096]{0:T(1024)S(1)} %copy-done.8, f32[512]{0:T(512)S(1)} %add_rsqrt_fusion), kind=kOutput, calls=%fused_computation.76 | convolution fusion | flops 2155872256 | bytes 9455616 | tf_op jit(solution)/shard_map/dot_general | solution.py:75
  67.5 1.4 copy.52
  68.8 1.3 copy.51
  71.4 1.4 subtract_convert_fusion
  73.7 7.1 %fusion.44 = f32[512,512]{1,0:T(8,128)} fusion(bf16[4096,512]{1,0:T(8,128)(2,1)} %param.17, bf16[512,4096]{1,0:T(8,128)(2,1)} %all-gather.3.cloned.1.call-done, f32[4096]{0:T(1024)S(1)} %copy-done.8, f32[512]{0:T(512)S(1)} %add_rsqrt_fusion), kind=kOutput, calls=%fused_computation.75 | convolution fusion | flops 2155872256 | bytes 9455616 | tf_op jit(solution)/shard_map/dot_general | solution.py:75
  80.8 6.4 %fusion.23 = bf16[1,512,512]{2,1,0:T(8,128)(2,1)S(1)} fusion(f32[512,512]{1,0:T(8,128)} %fusion.44, bf16[512,512]{1,0:T(8,128)(2,1)S(1)} %copy-done.7, bf16[4096,512]{1,0:T(8,128)(2,1)} %param.19, s32[512]{0:T(512)S(1)} %add_select_fusion, s32[512]{0:T(512)S(1)} %select_reduce_fusion, bf16[512,4096]{1,0:T(8,128)(2,1)} %all-gather.3.cloned.1.call-done, ...), kind=kOutput, calls=%fused_computation.36 | convolution fusion | flops 2425880576 | bytes 10508288 | tf_op jit(solution)/shard_map/dot_general | solution.py:85
  87.2 1.0 pad_maximum_fusion
  88.6 124.7 %all-gather.5.cloned.1.call-done = bf16[2,4096,512]{2,1,0:T(8,128)(2,1)} async-done(((bf16[2,512,512]{2,1,0:T(8,128)(2,1)}), bf16[2,4096,512]{2,1,0:T(8,128)(2,1)}) %all-gather.5.cloned.1.call-update) | async-done | bytes 8388624 | tf_op jit(solution)/shard_map/all_gather | solution.py:135
  213.3 55.8 %while.18 = (s32[]{:T(128)}, f32[4,512]{1,0:T(4,128)S(1)}, f32[4,512]{1,0:T(4,128)S(1)}, f32[4,512,128]{2,1,0:T(8,128)}, s32[512]{0:T(512)S(1)}, /*index=5*/bf16...) while((s32[]{:T(128)}, f32[4,512]{1,0:T(4,128)S(1)}, ...), condition=%wide.region_8.9_spmd.clone, body=%wide.region_5.8_spmd.clone.sunk | while | flops 552086528 | bytes 30026000 | solution.py:143
  213.6 1.3 constant_dynamic-slice_fusion.3
  217.4 1.8 fusion.76
  220.6 1.3 constant_dynamic-slice_fusion.3
  223.3 1.0 fusion.74
  224.4 1.8 fusion.76
  227.6 1.3 constant_dynamic-slice_fusion.3
  231.4 1.8 fusion.76
  234.6 1.3 constant_dynamic-slice_fusion.3
  238.4 1.8 fusion.76
  241.5 1.3 constant_dynamic-slice_fusion.3
  245.4 1.8 fusion.76
  248.5 1.3 constant_dynamic-slice_fusion.3
  252.3 1.8 fusion.76
  255.5 1.3 constant_dynamic-slice_fusion.3
  259.3 1.8 fusion.76
  262.5 1.3 constant_dynamic-slice_fusion.3
  266.3 1.8 fusion.76
  269.2 2.4 copy_bitcast_fusion
  (139 shorter events, 36.4 us)
Async XLA Ops:
  6.5 47.6 %copy-start = (bf16[512,512]{1,0:T(8,128)(2,1)S(1)}, bf16[512,512]{1,0:T(8,128)(2,1)}, u32[]{:S(2)}) copy-start(bf16[512,512]{1,0:T(8,128)(2,1)} %param.20) | copy-start | bytes 1572868
  6.5 42.8 %copy-start.8 = (f32[4096]{0:T(1024)S(1)}, f32[4096]{0:T(1024)}, u32[]{:S(2)}) copy-start(f32[4096]{0:T(1024)} %param.14) | copy-start | bytes 49156
  6.5 39.6 %all-gather.3.cloned.1.call-start = ((), (), s32[]{:S(2)}) async-start(), calls=%async_computation | async-start | bytes 5242880 | tf_op jit(solution)/shard_map/all_gather | solution.py:67
  7.3 206.1 %all-gather.5.cloned.1.call-start = ((), (), s32[]{:S(2)}) async-start(), calls=%async_computation.1 | async-start | bytes 9437184 | tf_op jit(solution)/shard_map/all_gather | solution.py:135
  46.1 3.4 %copy-start.1 = (bf16[512,4096]{1,0:T(8,128)(2,1)S(1)}, bf16[512,4096]{1,0:T(8,128)(2,1)}, u32[]{:S(2)}) copy-start(bf16[512,4096]{1,0:T(8,128)(2,1)} %all-gather.3.cloned.1.call-done) | copy-start | bytes 12582916
  70.2 1.2 copy-start.2
  70.2 1.3 copy-start.6
  73.7 7.1 %copy-start.7 = (bf16[512,512]{1,0:T(8,128)(2,1)S(1)}, bf16[512,512]{1,0:T(8,128)(2,1)}, u32[]{:S(2)}) copy-start(bf16[512,512]{1,0:T(8,128)(2,1)} %param.21) | copy-start | bytes 1572868
  80.8 7.5 %copy-start.3 = (bf16[512,4,64]{2,0,1:T(8,128)(2,1)S(1)}, bf16[512,4,64]{2,0,1:T(8,128)(2,1)}, u32[]{:S(2)}) copy-start(bf16[512,4,64]{2,0,1:T(8,128)(2,1)} %get-tuple-element.220) | copy-start | bytes 786436
  215.3 2.1 copy-start.4
  219.3 1.0 copy-start.5
  222.3 2.1 copy-start.4
  226.2 1.0 copy-start.5
  229.3 2.1 copy-start.4
  233.2 1.0 copy-start.5
  236.3 2.1 copy-start.4
  240.2 1.0 copy-start.5
  243.2 2.1 copy-start.4
  247.2 1.0 copy-start.5
  250.2 2.1 copy-start.4
  254.2 1.0 copy-start.5
  257.2 2.1 copy-start.4
  261.2 1.0 copy-start.5
  264.2 2.1 copy-start.4
  268.1 1.0 copy-start.5
Sparse Core Ops, SparseCore 0:
  8.9 37.1 all-gather.2
  88.4 124.9 all-gather.4
where the time goes:
time: 279 us; the launch traced here: 278 us
  waiting for transfers between devices  160 us (57%)
  matrix products  52.7 us (19%)
  local copies, waits for them, and re-layouts  27.9 us (10%)
  other arithmetic  23.4 us (8%)
  between operations  13.5 us (5%)
    all_gather x1, waiting for transfers between devices, body(): piece = lax.all_gather(key_value, 'req', axis=1, tiled=True)  125 us
    all_gather x1, waiting for transfers between devices, body(): whole = lax.all_gather(tokens, 'tp', axis=1, tiled=True)  34.7 us
    dot_general x3, matrix products, body(): jnp.dot(normed, weight, preferred_element_type=jnp.float32)  17.5 us
    dot_general x8, matrix products, attend(): jnp.einsum('hqk,khd->hqd', weights.astype(jnp.bfloat16), value_block, pre...  14.6 us
    while x56, local copies, waits for them, and re-layouts  11.7 us
    slice x8, local copies, waits for them, and re-layouts, attend(): value_block = block[1].reshape(block_rows, head_count, HEAD)  10.2 us
    reduce_sum x8, other arithmetic, attend(): new_total = total * factor + jnp.sum(weights, axis=2)  8.32 us
    dot_general x8, matrix products, attend(): jnp.einsum('hqd,khd->hqk', queries, key_block, preferred_element_type=jnp...  8.03 us
  transfers between devices with their start and end apart: 2, of which 2 were waited for; matrix products, arithmetic and copies ran while one was open for 2% of the time, Pallas kernels for 0%

commit v1 on v0

--- a/solution.py
+++ b/solution.py
@@ -3,6 +3,8 @@
 import jax
 import jax.numpy as jnp
 from jax import lax
+from jax.experimental import pallas as pl
+from jax.experimental.pallas import tpu as pltpu
 from jax.sharding import PartitionSpec as P
 
 HEAD = 128
@@ -146,6 +148,316 @@
     return jnp.transpose(attended, (1, 0, 2)).reshape(row_count, head_count * HEAD)
 
 
+LOG2E = 1.4426950408889634
+LAYERS = 4
+COLUMNS = 2
+
+
+def project_kernel(
+    scalars,
+    own,
+    near,
+    across,
+    far,
+    gain,
+    cosine,
+    sine,
+    prompt_mask,
+    query_w,
+    key_w,
+    value_w,
+    down,
+    query_up,
+    value_up,
+    out,
+    normed,
+    query_sum,
+    key_sum,
+    value_sum,
+    down_sum,
+):
+    step = pl.program_id(0)
+    blocks = (own, near, across, far)
+    rows = own.shape[0]
+    width = own.shape[1]
+
+    @pl.when(step == 0)
+    def _():
+        part = 32
+
+        def normalise(index, carry):
+            at = pl.ds(pl.multiple_of(index * part, part), part)
+            total = jnp.zeros((part, 1), jnp.float32)
+            for block in blocks:
+                value = block[at, :].astype(jnp.float32)
+                total += jnp.sum(value * value, axis=1, keepdims=True)
+            factor = lax.rsqrt(total / (len(blocks) * width) + EPS)
+            for number, block in enumerate(blocks):
+                value = block[at, :].astype(jnp.float32)
+                normed[number, at, :] = (value * factor * gain[number]).astype(jnp.bfloat16)
+            return carry
+
+        lax.fori_loop(0, rows // part, normalise, 0)
+        query_sum[...] = jnp.zeros_like(query_sum)
+        key_sum[...] = jnp.zeros_like(key_sum)
+        value_sum[...] = jnp.zeros_like(value_sum)
+        down_sum[...] = jnp.zeros_like(down_sum)
+
+    tile = normed[step]
+    query_sum[...] += jnp.dot(tile, query_w[...], preferred_element_type=jnp.float32)
+    key_sum[...] += jnp.dot(tile, key_w[...], preferred_element_type=jnp.float32)
+    value_sum[...] += jnp.dot(tile, value_w[...], preferred_element_type=jnp.float32)
+    down_sum[...] += jnp.dot(tile, down[...], preferred_element_type=jnp.float32)
+
+    @pl.when(step == len(blocks) - 1)
+    def _():
+        layer = scalars[1]
+        middle = (down_sum[...] * prompt_mask[...]).astype(jnp.bfloat16)
+        for head in range(LAYERS):
+            place = lax.rem(head - layer + LAYERS, LAYERS)
+            lanes = slice(head * HEAD, (head + 1) * HEAD)
+            query = query_sum[:, lanes] + ADAPTER_SCALE * jnp.dot(
+                middle, query_up[:, lanes], preferred_element_type=jnp.float32
+            )
+            key = key_sum[:, lanes]
+            value = value_sum[:, lanes] + ADAPTER_SCALE * jnp.dot(
+                middle, value_up[:, lanes], preferred_element_type=jnp.float32
+            )
+            for slot, field in enumerate((query, key)):
+                turned = field * cosine[...] + pltpu.roll(field, HEAD // 2, 1) * sine[...]
+                out[place, slot] = turned.astype(jnp.bfloat16)
+            out[place, 2] = value.astype(jnp.bfloat16)
+
+
+def attend_kernel(scalars, mine, other, out, peak, total, summed):
+    step = pl.program_id(0)
+    rows = mine.shape[2]
+    layer, column = scalars[0], scalars[1]
+    prompts = scalars.shape[0] - 2
+    query_block = lax.rem(layer - step + LAYERS, LAYERS) * COLUMNS + column
+    first = query_block * rows
+    last = first + rows - 1
+    end = 0
+    first_start = 0
+    last_start = 0
+    for prompt in range(prompts):
+        length = scalars[2 + prompt]
+        end = end + length
+        first_start += jnp.where(end <= first, length, 0)
+        last_start += jnp.where(end <= last, length, 0)
+    query = mine[step, 0]
+    peak[...] = jnp.full_like(peak, MASKED)
+    total[...] = jnp.zeros_like(total)
+    summed[...] = jnp.zeros_like(summed)
+    scale = LOG2E / math.sqrt(HEAD)
+
+    def visit(block, masked, key, value):
+        scores = (
+            lax.dot_general(
+                query, key, (((1,), (1,)), ((), ())), preferred_element_type=jnp.float32
+            )
+            * scale
+        )
+        if masked:
+            position = first + lax.broadcasted_iota(jnp.int32, (rows, 1), 0)
+            start = jnp.zeros((rows, 1), jnp.int32)
+            ending = 0
+            for prompt in range(prompts):
+                length = scalars[2 + prompt]
+                ending = ending + length
+                start += jnp.where(position >= ending, length, 0)
+            key_position = block * rows + lax.broadcasted_iota(jnp.int32, (1, rows), 1)
+            allowed = (key_position >= start) & (key_position <= position)
+            scores = jnp.where(allowed, scores, MASKED)
+        new_peak = jnp.maximum(peak[...], jnp.max(scores, axis=1, keepdims=True))
+        weights = jnp.exp2(scores - new_peak)
+        if masked:
+            weights = jnp.where(allowed, weights, 0.0)
+        factor = jnp.exp2(peak[...] - new_peak)
+        total[...] = total[...] * factor + jnp.sum(weights, axis=1, keepdims=True)
+        summed[...] = summed[...] * factor + jnp.dot(
+            weights.astype(jnp.bfloat16), value, preferred_element_type=jnp.float32
+        )
+        peak[...] = new_peak
+
+    def turn(block, carry):
+        key_layer = block // COLUMNS
+        place = lax.rem(layer - key_layer + LAYERS, LAYERS)
+        same = lax.rem(block, COLUMNS) == column
+        whole = (block < query_block) & (block * rows >= last_start)
+        for is_mine in (True, False):
+            for masked in (True, False):
+
+                @pl.when((same == is_mine) & (whole != masked))
+                def _():
+                    if is_mine:
+                        visit(block, masked, mine[place, 1], mine[place, 2])
+                    else:
+                        visit(block, masked, other[place, 0], other[place, 1])
+
+        return carry
+
+    lax.fori_loop(first_start // rows, query_block + 1, turn, 0)
+    out[0] = (summed[...] / total[...]).astype(jnp.bfloat16)
+
+
+def fast_body(
+    tokens,
+    input_norm_gain,
+    query_weight,
+    key_weight,
+    value_weight,
+    query_down_maps,
+    value_down_maps,
+    query_up_maps,
+    value_up_maps,
+    lengths,
+    prompt_adapter_index,
+):
+    row_count, width = tokens.shape
+    depth = query_weight.shape[0]
+    features = query_weight.shape[1]
+    prompts = lengths.shape[0]
+    req_index = lax.axis_index("req")
+    tp_index = lax.axis_index("tp")
+    layer = req_index // COLUMNS
+    column = lax.rem(req_index, COLUMNS)
+    peers = depth // width
+
+    def flip(array, bit):
+        return lax.ppermute(array, "tp", [(i, i ^ bit) for i in range(peers)])
+
+    across = flip(tokens, 2)
+    near = flip(tokens, 1)
+    far = flip(across, 1)
+
+    positions = req_index * row_count + jnp.arange(row_count, dtype=jnp.int32)
+    starts, prompt = prompt_layout(lengths, positions)
+    lane = jnp.arange(2 * prompts * ADAPTER_RANK, dtype=jnp.int32)
+    lane_prompt = lax.rem(lane // ADAPTER_RANK, prompts)
+    prompt_mask = (prompt[:, None] == lane_prompt[None, :]).astype(jnp.float32)
+    half = HEAD // 2
+    freq = jnp.exp(jnp.arange(half, dtype=jnp.float32) * (-2.0 * math.log(10000.0) / HEAD))
+    angle = (positions - starts).astype(jnp.float32)[:, None] * freq[None, :]
+    cosine = jnp.cos(angle)
+    sine = jnp.sin(angle)
+    cosine = jnp.concatenate([cosine, cosine], axis=1)
+    sine = jnp.concatenate([-sine, sine], axis=1)
+    chosen = jnp.sum(
+        (lane_prompt[:, None] == jnp.arange(prompts)[None, :]) * prompt_adapter_index[None, :],
+        axis=1,
+    ) * ADAPTER_RANK + lax.rem(lane, ADAPTER_RANK)
+    pick = chosen[None, :] == jnp.arange(query_down_maps.shape[1])[:, None]
+    is_query = lane < prompts * ADAPTER_RANK
+    pick_query = (pick & is_query[None, :]).astype(jnp.bfloat16)
+    pick_value = (pick & ~is_query[None, :]).astype(jnp.bfloat16)
+    down = (
+        jnp.dot(query_down_maps, pick_query, preferred_element_type=jnp.float32)
+        + jnp.dot(value_down_maps, pick_value, preferred_element_type=jnp.float32)
+    ).astype(jnp.bfloat16)
+    query_up = jnp.dot(
+        pick_query.T, query_up_maps, preferred_element_type=jnp.float32
+    ).astype(jnp.bfloat16)
+    value_up = jnp.dot(
+        pick_value.T, value_up_maps, preferred_element_type=jnp.float32
+    ).astype(jnp.bfloat16)
+    order = tp_index ^ jnp.arange(peers, dtype=jnp.int32)
+    gain = input_norm_gain.reshape(peers, 1, width)[order]
+
+    def full(shape):
+        return pl.BlockSpec(shape, lambda j, s: (0,) * len(shape))
+
+    def weight(columns):
+        return pl.BlockSpec((width, columns), lambda j, s: (s[0] ^ j, 0))
+
+    projected = pl.pallas_call(
+        project_kernel,
+        grid_spec=pltpu.PrefetchScalarGridSpec(
+            num_scalar_prefetch=1,
+            grid=(peers,),
+            in_specs=[full((row_count, width))] * 4
+            + [full((peers, 1, width))]
+            + [full((row_count, HEAD))] * 2
+            + [full((row_count, lane.shape[0]))]
+            + [weight(features)] * 3
+            + [weight(lane.shape[0])]
+            + [full((lane.shape[0], features))] * 2,
+            out_specs=full((LAYERS, 3, row_count, HEAD)),
+            scratch_shapes=[pltpu.VMEM((peers, row_count, width), jnp.bfloat16)]
+            + [pltpu.VMEM((row_count, features), jnp.float32)] * 3
+            + [pltpu.VMEM((row_count, lane.shape[0]), jnp.float32)],
+        ),
+        out_shape=jax.ShapeDtypeStruct((LAYERS, 3, row_count, HEAD), jnp.bfloat16),
+        compiler_params=pltpu.CompilerParams(vmem_limit_bytes=48 * 1024 * 1024),
+        name="project",
+    )(
+        jnp.stack([tp_index, layer]).astype(jnp.int32),
+        tokens,
+        near,
+        across,
+        far,
+        gain,
+        cosine,
+        sine,
+        prompt_mask,
+        query_weight,
+        key_weight,
+        value_weight,
+        down,
+        query_up,
+        value_up,
+    )
+
+    def along(array, distance):
+        pairs = [
+            (z * COLUMNS + y, (z + distance) % LAYERS * COLUMNS + y)
+            for z in range(LAYERS)
+            for y in range(COLUMNS)
+        ]
+        return lax.ppermute(array, "req", pairs)
+
+    def swap(array):
+        return lax.ppermute(array, "req", [(i, i ^ 1) for i in range(LAYERS * COLUMNS)])
+
+    mine = [projected[0]]
+    mine_kv = {s: along(projected[s, 1:], s) for s in (2, 1, 3)}
+    mine_q = {s: along(projected[s, :1], s) for s in (2, 1, 3)}
+    other = [swap(projected[0, 1:])] + [swap(mine_kv[s]) for s in range(1, LAYERS)]
+    mine = jnp.stack(
+        [projected[0]]
+        + [jnp.concatenate([mine_q[s], mine_kv[s]], axis=0) for s in range(1, LAYERS)]
+    )
+    other = jnp.stack(other)
+    attended = pl.pallas_call(
+        attend_kernel,
+        grid_spec=pltpu.PrefetchScalarGridSpec(
+            num_scalar_prefetch=1,
+            grid=(LAYERS,),
+            in_specs=[
+                full((LAYERS, 3, row_count, HEAD)),
+                full((LAYERS, 2, row_count, HEAD)),
+            ],
+            out_specs=pl.BlockSpec((1, row_count, HEAD), lambda j, s: (j, 0, 0)),
+            scratch_shapes=[
+                pltpu.VMEM((row_count, 1), jnp.float32),
+                pltpu.VMEM((row_count, 1), jnp.float32),
+                pltpu.VMEM((row_count, HEAD), jnp.float32),
+            ],
+        ),
+        out_shape=jax.ShapeDtypeStruct((LAYERS, row_count, HEAD), jnp.bfloat16),
+        compiler_params=pltpu.CompilerParams(vmem_limit_bytes=48 * 1024 * 1024),
+        name="attend",
+    )(
+        jnp.concatenate([jnp.stack([layer, column]).astype(jnp.int32), lengths]),
+        mine,
+        other,
+    )
+    parts = [attended[0]] + [along(attended[s], LAYERS - s) for s in range(1, LAYERS)]
+    parts = jnp.stack(parts)
+    slots = lax.rem(jnp.arange(LAYERS, dtype=jnp.int32) - layer + LAYERS, LAYERS)
+    return jnp.concatenate([parts[slots[h]] for h in range(LAYERS)], axis=1)
+
+
 def solution(mesh):
     in_specs = (
         P("req", "tp"),
@@ -161,4 +473,8 @@
         P(),
     )
     out_specs = P("req", "tp")
-    return jax.shard_map(body, mesh=mesh, in_specs=in_specs, out_specs=out_specs, check_vma=False)
+    fast = mesh.shape["req"] == LAYERS * COLUMNS and mesh.shape["tp"] == 4
+    chosen = fast_body if fast else body
+    return jax.shard_map(
+        chosen, mesh=mesh, in_specs=in_specs, out_specs=out_specs, check_vma=False
+    )

time: 279 us -> 146 us (0.52)
  waiting for transfers between devices: 160 us -> 62.2 us
  matrix products: 52.7 us -> 7.45 us
  Pallas kernels: 0 us -> 31.7 us
  starting transfers between devices: 0.04 us -> 23.1 us
  local copies, waits for them, and re-layouts: 27.9 us -> 6.13 us
  other arithmetic: 23.4 us -> 5.71 us
  between operations: 13.5 us -> 7.81 us
    all_gather x2 -> x0, waiting for transfers between devices: 159 us -> none  [the longest x1 125 us: body(): piece = lax.all_gather(key_value, 'req', axis=1, tiled=True)]
    ppermute x0 -> x16, waiting for transfers between devices: none -> 62.2 us  [the longest x9 27.8 us: along(): return lax.ppermute(array, 'req', pairs)]
    dot_general x21 -> x4, matrix products: 52.7 us -> 7.45 us  [the longest x1 3.61 us: fast_body(): jnp.dot(query_down_maps, pick_query, preferred_element_type=jnp.float32)]
    pallas_call x0 -> x2, Pallas kernels: none -> 31.7 us  [the longest x1 16.6 us: fast_body(): pl.pallas_call(project_kernel, grid_spec=pltpu.PrefetchScalarGridSpec(num...]
    ppermute x0 -> x16, starting transfers between devices: none -> 23.1 us  [the longest x9 14.9 us: along(): return lax.ppermute(array, 'req', pairs)]
    while x56 -> x0, local copies, waits for them, and re-layouts: 11.7 us -> none
    reduce_sum x10 -> x1, other arithmetic: 12.3 us -> 0.74 us  [fast_body(): jnp.sum((lane_prompt[:, None] == jnp.arange(prompts)[None, :]) * prompt_a...]
    slice x10 -> x4, local copies, waits for them, and re-layouts: 11.7 us -> 0.71 us  [the longest x1 0.66 us: fast_body(): return jnp.concatenate([parts[slots[h]] for h in range(LAYERS)], axis=1)]
  transfers between devices with their start and end apart: 2 -> 16, of which waited for: 2 -> 7; matrix products, arithmetic and copies ran while one was open for 2% -> 12% of each run, Pallas kernels for 0% -> 0%
where the time goes in v1:
time: 146 us; the launch traced here: 144 us
  waiting for transfers between devices  62.2 us (43%)
  Pallas kernels  31.7 us (22%)
  starting transfers between devices  23.1 us (16%)
  between operations  7.81 us (5%)
  matrix products  7.45 us (5%)
  local copies, waits for them, and re-layouts  6.13 us (4%)
  other arithmetic  5.71 us (4%)
    ppermute x9, waiting for transfers between devices, along(): return lax.ppermute(array, 'req', pairs)  27.8 us
    ppermute x3, waiting for transfers between devices, flip(): return lax.ppermute(array, 'tp', [(i, i ^ bit) for i in range(peers)])  18.8 us
    pallas_call x1, Pallas kernels, fast_body(): pl.pallas_call(project_kernel, grid_spec=pltpu.PrefetchScalarGridSpec(num...  16.6 us
    ppermute x4, waiting for transfers between devices, swap(): lax.ppermute(array, 'req', [(i, i ^ 1) for i in range(LAYERS * COLUMNS)])  15.6 us
    pallas_call x1, Pallas kernels, fast_body(): pl.pallas_call(attend_kernel, grid_spec=pltpu.PrefetchScalarGridSpec(num_...  15.1 us
    ppermute x9, starting transfers between devices, along(): return lax.ppermute(array, 'req', pairs)  14.9 us
    ppermute x4, starting transfers between devices, swap(): lax.ppermute(array, 'req', [(i, i ^ 1) for i in range(LAYERS * COLUMNS)])  5.23 us
    dot_general x1, matrix products, fast_body(): jnp.dot(query_down_maps, pick_query, preferred_element_type=jnp.float32)  3.61 us
  transfers between devices with their start and end apart: 16, of which 7 were waited for; matrix products, arithmetic and copies ran while one was open for 12% of the time, Pallas kernels for 0%

profile of v1, /device:TPU:0, one launch (start us, length us, event | category | flops | bytes accessed | tf_op | source)
XLA Modules:
  0.0 144.0 jit_solution(8220099303402205615)
XLA Ops:
  0.0 2.9 %collective-permute-start.1 = (bf16[512,1024]{1,0:T(8,128)(2,1)}, bf16[512,1024]{1,0:T(8,128)(2,1)S(1)}, u32[]{:S(2)}, u32[]{:S(2)}) collective-permute-start(bf16[512,1024]{1,0:T(8,128)(2,1)} %own.1), channel_id=1, source_target_pairs={{0,2},{1,3},{2,0},{3,1},{4,6},{5,7},{6,4},{7,5},{8,10},{9,11},{10,... | collective-permute-start | bytes 3145736 | tf_op jit(solution)/shard_map/ppermute | solution.py:328
  3.5 0.8 reduce-window.8
  4.3 0.7 fusion.19
  5.1 0.7 select_reduce_fusion
  5.8 1.0 fusion.17
  7.5 18.8 %collective-permute-done.1.across = bf16[512,1024]{1,0:T(8,128)(2,1)S(1)} collective-permute-done((bf16[512,1024]{1,0:T(8,128)(2,1)}, bf16[512,1024]{1,0:T(8,128)(2,1)S(1)}, u32[]{:S(2)}, u32[]{:S(2)}) %collective-permute-start.1) | collective-permute-done | bytes 1048608 | tf_op jit(solution)/shard_map/ppermute | solution.py:328
  26.4 1.3 reshape.116
  27.7 1.9 %gather_fusion = f32[4,1024]{1,0:T(4,128)} fusion(f32[4,1024]{1,0:T(4,128)} %reshape.116, s32[1024]{0:T(1024)S(1)} %pad_clamp_fusion), kind=kCustom, calls=%fused_computation | custom fusion | bytes 32784 | tf_op jit(solution)/shard_map/gather | solution.py:365
  29.6 0.7 reshape.117.gain
  30.3 1.3 convolution_convert_fusion.1.query_up
  31.7 3.6 %fusion.5 = f32[128,4096]{0,1:T(8,128)S(1)} fusion(bf16[4096,512]{1,0:T(8,128)(2,1)} %param.16, s32[128]{0:T(128)S(1)} %fusion.20, pred[128]{0:T(512)(128)(4,1)} %iota_compare_fusion.2), kind=kOutput, calls=%fused_computation.24 | convolution fusion | flops 537001984 | bytes 6292096 | tf_op jit(solution)/shard_map/dot_general | solution.py:355
  35.3 2.2 %fusion.1.down = bf16[4096,128]{1,0:T(8,128)(2,1)} fusion(f32[128,4096]{0,1:T(8,128)S(1)} %fusion.5, bf16[4096,512]{1,0:T(8,128)(2,1)S(1)} %copy-done.3, s32[128]{0:T(128)S(1)} %fusion.20, pred[128]{0:T(512)(128)(4,1)S(1)} %fusion.24), kind=kOutput, calls=%fused_computation.3 | convolution fusion | flops 538050560 | bytes 7340672 | tf_op jit(solution)/shard_map/dot_general | solution.py:356
  37.6 16.6 %project.1 = bf16[4,3,512,128]{3,2,1,0:T(8,128)(2,1)} custom-call(s32[2]{0:T(128)S(1)} %pad_add_fusion.1.scalars, bf16[512,1024]{1,0:T(8,128)(2,1)S(1)} %copy-done.1, bf16[512,1024]{1,0:T(8,128)(2,1)S(1)} %collective-permute-done.near, bf16[512,1024]{1,0:T(8,128)(2,1)S(1)} %collective-permute-done.1.across, bf16[512,1024]{1,0:T(8,128)(2,1)} %collective-permute-done.2.far, ...), custom_call_target="tpu_custom_call" | custom-call | tf_op jit(solution)/shard_map/project/pallas_call | solution.py:373
  54.2 1.4 slice_bitcast_fusion
  55.6 1.9 %collective-permute-start.4 = (bf16[2,512,128]{2,1,0:T(8,128)(2,1)S(1)}, bf16[2,512,128]{2,1,0:T(8,128)(2,1)S(1)}, u32[]{:S(2)}, u32[]{:S(2)}) collective-permute-start(bf16[2,512,128]{2,1,0:T(8,128)(2,1)S(1)} %get-tuple-element.10), channel_id=1, source_target_pairs={{0,8},{4,12},{8,16},{12,20},{16,24},{20,28},{24,0},{28,4},{1,9},{5... | collective-permute-start | bytes 786440 | tf_op jit(solution)/shard_map/ppermute | solution.py:417
  57.4 2.6 %collective-permute-start.6 = (bf16[2,512,128]{2,1,0:T(8,128)(2,1)S(1)}, bf16[2,512,128]{2,1,0:T(8,128)(2,1)S(1)}, u32[]{:S(2)}, u32[]{:S(2)}) collective-permute-start(bf16[2,512,128]{2,1,0:T(8,128)(2,1)S(1)} %get-tuple-element.9), channel_id=1, source_target_pairs={{0,16},{4,20},{8,24},{12,28},{16,0},{20,4},{24,8},{28,12},{1,17},{... | collective-permute-start | bytes 786440 | tf_op jit(solution)/shard_map/ppermute | solution.py:417
  60.0 1.3 collective-permute-start.8
  61.4 0.7 collective-permute-start.3
  62.6 18.3 %collective-permute-done.3 = bf16[1,512,128]{2,1,0:T(8,128)(2,1)S(1)} collective-permute-done((bf16[1,512,128]{2,1,0:T(8,128)(2,1)S(1)}, bf16[1,512,128]{2,1,0:T(8,128)(2,1)S(1)}, u32[]{:S(2)}, u32[]{:S(2)}) %collective-permute-start.3) | collective-permute-done | bytes 131104 | tf_op jit(solution)/shard_map/ppermute | solution.py:417
  80.9 1.6 %collective-permute-start.9 = (bf16[2,512,128]{2,1,0:T(8,128)(2,1)S(1)}, bf16[2,512,128]{2,1,0:T(8,128)(2,1)S(1)}, u32[]{:S(2)}, u32[]{:S(2)}) collective-permute-start(bf16[2,512,128]{2,1,0:T(8,128)(2,1)S(1)} %get-tuple-element.7), channel_id=1, source_target_pairs={{0,4},{4,0},{8,12},{12,8},{16,20},{20,16},{24,28},{28,24},{1,5},{5... | collective-permute-start | bytes 786440 | tf_op jit(solution)/shard_map/ppermute | solution.py:420
  82.5 9.2 %collective-permute-done.5 = bf16[1,512,128]{2,1,0:T(8,128)(2,1)S(1)} collective-permute-done((bf16[1,512,128]{2,1,0:T(8,128)(2,1)S(1)}, bf16[1,512,128]{2,1,0:T(8,128)(2,1)S(1)}, u32[]{:S(2)}, u32[]{:S(2)}) %collective-permute-start.5) | collective-permute-done | bytes 131104 | tf_op jit(solution)/shard_map/ppermute | solution.py:417
  91.8 1.6 %collective-permute-start.10 = (bf16[2,512,128]{2,1,0:T(8,128)(2,1)S(1)}, bf16[2,512,128]{2,1,0:T(8,128)(2,1)S(1)}, u32[]{:S(2)}, u32[]{:S(2)}) collective-permute-start(bf16[2,512,128]{2,1,0:T(8,128)(2,1)S(1)} %collective-permute-done.4), channel_id=1, source_target_pairs={{0,4},{4,0},{8,12},{12,8},{16,20},{20,16},{24,28},{28,24},{1,5},{5... | collective-permute-start | bytes 786440 | tf_op jit(solution)/shard_map/ppermute | solution.py:420
  93.8 1.6 %collective-permute-start.12 = (bf16[2,512,128]{2,1,0:T(8,128)(2,1)S(1)}, bf16[2,512,128]{2,1,0:T(8,128)(2,1)S(1)}, u32[]{:S(2)}, u32[]{:S(2)}) collective-permute-start(bf16[2,512,128]{2,1,0:T(8,128)(2,1)S(1)} %collective-permute-done.8), channel_id=1, source_target_pairs={{0,4},{4,0},{8,12},{12,8},{16,20},{20,16},{24,28},{28,24},{1,5},{5... | collective-permute-start | bytes 786440 | tf_op jit(solution)/shard_map/ppermute | solution.py:420
  95.7 5.2 %collective-permute-done.10 = bf16[2,512,128]{2,1,0:T(8,128)(2,1)S(1)} collective-permute-done((bf16[2,512,128]{2,1,0:T(8,128)(2,1)S(1)}, bf16[2,512,128]{2,1,0:T(8,128)(2,1)S(1)}, u32[]{:S(2)}, u32[]{:S(2)}) %collective-permute-start.10) | collective-permute-done | bytes 262176 | tf_op jit(solution)/shard_map/ppermute | solution.py:420
  100.9 5.6 %collective-permute-done.11 = bf16[2,512,128]{2,1,0:T(8,128)(2,1)S(1)} collective-permute-done((bf16[2,512,128]{2,1,0:T(8,128)(2,1)S(1)}, bf16[2,512,128]{2,1,0:T(8,128)(2,1)S(1)}, u32[]{:S(2)}, u32[]{:S(2)}) %collective-permute-start.11) | collective-permute-done | bytes 262176 | tf_op jit(solution)/shard_map/ppermute | solution.py:420
  106.5 4.7 %collective-permute-done.12 = bf16[2,512,128]{2,1,0:T(8,128)(2,1)S(1)} collective-permute-done((bf16[2,512,128]{2,1,0:T(8,128)(2,1)S(1)}, bf16[2,512,128]{2,1,0:T(8,128)(2,1)S(1)}, u32[]{:S(2)}, u32[]{:S(2)}) %collective-permute-start.12) | collective-permute-done | bytes 262176 | tf_op jit(solution)/shard_map/ppermute | solution.py:420
  111.4 15.1 %attend.1 = bf16[4,512,128]{2,1,0:T(8,128)(2,1)S(1)} custom-call(s32[6]{0:T(128)S(1)} %pad_add_fusion.scalars, bf16[4,3,512,128]{3,2,1,0:T(8,128)(2,1)S(1)} %pad_maximum_fusion.mine, bf16[4,2,512,128]{3,2,1,0:T(8,128)(2,1)S(1)} %pad_maximum_fusion.1.other), custom_call_target="tpu_custom_call" | custom-call | tf_op jit(solution)/shard_map/attend/pallas_call | solution.py:431
  126.5 4.1 %collective-permute-start.13 = (bf16[512,128]{1,0:T(8,128)(2,1)S(1)}, bf16[512,128]{1,0:T(8,128)(2,1)S(1)}, u32[]{:S(2)}, u32[]{:S(2)}) collective-permute-start(bf16[512,128]{1,0:T(8,128)(2,1)S(1)} %get-tuple-element.21), channel_id=1, source_target_pairs={{0,24},{4,28},{8,0},{12,4},{16,8},{20,12},{24,16},{28,20},{1,25},{... | collective-permute-start | bytes 393224 | tf_op jit(solution)/shard_map/ppermute | solution.py:417
  130.6 2.0 %collective-permute-start.14 = (bf16[512,128]{1,0:T(8,128)(2,1)S(1)}, bf16[512,128]{1,0:T(8,128)(2,1)S(1)}, u32[]{:S(2)}, u32[]{:S(2)}) collective-permute-start(bf16[512,128]{1,0:T(8,128)(2,1)S(1)} %get-tuple-element.20), channel_id=1, source_target_pairs={{0,16},{4,20},{8,24},{12,28},{16,0},{20,4},{24,8},{28,12},{1,17},{... | collective-permute-start | bytes 393224 | tf_op jit(solution)/shard_map/ppermute | solution.py:417
  132.6 1.9 %collective-permute-start.15 = (bf16[512,128]{1,0:T(8,128)(2,1)S(1)}, bf16[512,128]{1,0:T(8,128)(2,1)S(1)}, u32[]{:S(2)}, u32[]{:S(2)}) collective-permute-start(bf16[512,128]{1,0:T(8,128)(2,1)S(1)} %get-tuple-element.19), channel_id=1, source_target_pairs={{0,8},{4,12},{8,16},{12,20},{16,24},{20,28},{24,0},{28,4},{1,9},{5... | collective-permute-start | bytes 393224 | tf_op jit(solution)/shard_map/ppermute | solution.py:417
  134.6 0.7 fusion.26
  143.2 0.9 pad_maximum_fusion.3
  (51 shorter events, 3.0 us)
Async XLA Ops:
  0.0 7.2 %copy-start = (bf16[512,512]{1,0:T(8,128)(2,1)S(1)}, bf16[512,512]{1,0:T(8,128)(2,1)}, u32[]{:S(2)}) copy-start(bf16[512,512]{1,0:T(8,128)(2,1)} %param.19) | copy-start | bytes 1572868
  0.0 26.3 %collective-permute-start.1 = (bf16[512,1024]{1,0:T(8,128)(2,1)}, bf16[512,1024]{1,0:T(8,128)(2,1)S(1)}, u32[]{:S(2)}, u32[]{:S(2)}) collective-permute-start(bf16[512,1024]{1,0:T(8,128)(2,1)} %own.1), channel_id=1, source_target_pairs={{0,2},{1,3},{2,0},{3,1},{4,6},{5,7},{6,4},{7,5},{8,10},{9,11},{10,... | collective-permute-start | bytes 3145736 | tf_op jit(solution)/shard_map/ppermute | solution.py:328
  2.9 34.6 %collective-permute-start = (bf16[512,1024]{1,0:T(8,128)(2,1)}, bf16[512,1024]{1,0:T(8,128)(2,1)S(1)}, u32[]{:S(2)}, u32[]{:S(2)}) collective-permute-start(bf16[512,1024]{1,0:T(8,128)(2,1)} %own.1), channel_id=1, source_target_pairs={{0,1},{1,0},{2,3},{3,2},{4,5},{5,4},{6,7},{7,6},{8,9},{9,8},{10,11... | collective-permute-start | bytes 3145736 | tf_op jit(solution)/shard_map/ppermute | solution.py:328
  26.3 11.3 %collective-permute-start.2 = (bf16[512,1024]{1,0:T(8,128)(2,1)S(1)}, bf16[512,1024]{1,0:T(8,128)(2,1)}, u32[]{:S(2)}, u32[]{:S(2)}) collective-permute-start(bf16[512,1024]{1,0:T(8,128)(2,1)S(1)} %collective-permute-done.1.across), channel_id=1, source_target_pairs={{0,1},{1,0},{2,3},{3,2},{4,5},{5,4},{6,7},{7,6},{8,9},{9,8},{10,11... | collective-permute-start | bytes 3145736 | tf_op jit(solution)/shard_map/ppermute | solution.py:328
  31.7 3.6 %copy-start.3 = (bf16[4096,512]{1,0:T(8,128)(2,1)S(1)}, bf16[4096,512]{1,0:T(8,128)(2,1)}, u32[]{:S(2)}) copy-start(bf16[4096,512]{1,0:T(8,128)(2,1)} %param.17) | copy-start | bytes 12582916
  35.3 2.3 %copy-start.1 = (bf16[512,1024]{1,0:T(8,128)(2,1)S(1)}, bf16[512,1024]{1,0:T(8,128)(2,1)}, u32[]{:S(2)}) copy-start(bf16[512,1024]{1,0:T(8,128)(2,1)} %own.1) | copy-start | bytes 3145732
  54.2 7.2 %copy-start.2 = (bf16[4,3,512,128]{3,2,1,0:T(8,128)(2,1)S(1)}, bf16[4,3,512,128]{3,2,1,0:T(8,128)(2,1)}, u32[]{:S(2)}) copy-start(bf16[4,3,512,128]{3,2,1,0:T(8,128)(2,1)} %project.1) | copy-start | bytes 4718596
  54.2 8.3 %copy-start.4 = (s32[4]{0:T(128)S(1)}, s32[4]{0:T(128)}, u32[]{:S(2)}) copy-start(s32[4]{0:T(128)} %param.20) | copy-start | bytes 52
  55.5 39.9 %slice-start = ((bf16[4,3,512,128]{3,2,1,0:T(8,128)(2,1)}), bf16[1,3,512,128]{3,2,1,0:T(8,128)(2,1)S(1)}, s32[]{:S(2)}) async-start(bf16[4,3,512,128]{3,2,1,0:T(8,128)(2,1)} %project.1), calls=%async_computation | async-start | bytes 786432 | tf_op jit(solution)/shard_map/slice | solution.py:427
  55.6 26.9 %collective-permute-start.4 = (bf16[2,512,128]{2,1,0:T(8,128)(2,1)S(1)}, bf16[2,512,128]{2,1,0:T(8,128)(2,1)S(1)}, u32[]{:S(2)}, u32[]{:S(2)}) collective-permute-start(bf16[2,512,128]{2,1,0:T(8,128)(2,1)S(1)} %get-tuple-element.10), channel_id=1, source_target_pairs={{0,8},{4,12},{8,16},{12,20},{16,24},{20,28},{24,0},{28,4},{1,9},{5... | collective-permute-start | bytes 786440 | tf_op jit(solution)/shard_map/ppermute | solution.py:417
  57.4 35.9 %collective-permute-start.6 = (bf16[2,512,128]{2,1,0:T(8,128)(2,1)S(1)}, bf16[2,512,128]{2,1,0:T(8,128)(2,1)S(1)}, u32[]{:S(2)}, u32[]{:S(2)}) collective-permute-start(bf16[2,512,128]{2,1,0:T(8,128)(2,1)S(1)} %get-tuple-element.9), channel_id=1, source_target_pairs={{0,16},{4,20},{8,24},{12,28},{16,0},{20,4},{24,8},{28,12},{1,17},{... | collective-permute-start | bytes 786440 | tf_op jit(solution)/shard_map/ppermute | solution.py:417
  60.0 33.8 %collective-permute-start.8 = (bf16[2,512,128]{2,1,0:T(8,128)(2,1)S(1)}, bf16[2,512,128]{2,1,0:T(8,128)(2,1)S(1)}, u32[]{:S(2)}, u32[]{:S(2)}) collective-permute-start(bf16[2,512,128]{2,1,0:T(8,128)(2,1)S(1)} %get-tuple-element.8), channel_id=1, source_target_pairs={{0,24},{4,28},{8,0},{12,4},{16,8},{20,12},{24,16},{28,20},{1,25},{... | collective-permute-start | bytes 786440 | tf_op jit(solution)/shard_map/ppermute | solution.py:417
  61.4 19.4 %collective-permute-start.3 = (bf16[1,512,128]{2,1,0:T(8,128)(2,1)S(1)}, bf16[1,512,128]{2,1,0:T(8,128)(2,1)S(1)}, u32[]{:S(2)}, u32[]{:S(2)}) collective-permute-start(bf16[1,512,128]{2,1,0:T(8,128)(2,1)S(1)} %get-tuple-element.11), channel_id=1, source_target_pairs={{0,8},{4,12},{8,16},{12,20},{16,24},{20,28},{24,0},{28,4},{1,9},{5... | collective-permute-start | bytes 393224 | tf_op jit(solution)/shard_map/ppermute | solution.py:417
  62.1 29.6 %collective-permute-start.5 = (bf16[1,512,128]{2,1,0:T(8,128)(2,1)S(1)}, bf16[1,512,128]{2,1,0:T(8,128)(2,1)S(1)}, u32[]{:S(2)}, u32[]{:S(2)}) collective-permute-start(bf16[1,512,128]{2,1,0:T(8,128)(2,1)S(1)} %get-tuple-element.13), channel_id=1, source_target_pairs={{0,16},{4,20},{8,24},{12,28},{16,0},{20,4},{24,8},{28,12},{1,17},{... | collective-permute-start | bytes 393224 | tf_op jit(solution)/shard_map/ppermute | solution.py:417
  80.9 14.8 %collective-permute-start.9 = (bf16[2,512,128]{2,1,0:T(8,128)(2,1)S(1)}, bf16[2,512,128]{2,1,0:T(8,128)(2,1)S(1)}, u32[]{:S(2)}, u32[]{:S(2)}) collective-permute-start(bf16[2,512,128]{2,1,0:T(8,128)(2,1)S(1)} %get-tuple-element.7), channel_id=1, source_target_pairs={{0,4},{4,0},{8,12},{12,8},{16,20},{20,16},{24,28},{28,24},{1,5},{5... | collective-permute-start | bytes 786440 | tf_op jit(solution)/shard_map/ppermute | solution.py:420
  82.5 12.9 %collective-permute-start.7 = (bf16[1,512,128]{2,1,0:T(8,128)(2,1)S(1)}, bf16[1,512,128]{2,1,0:T(8,128)(2,1)S(1)}, u32[]{:S(2)}, u32[]{:S(2)}) collective-permute-start(bf16[1,512,128]{2,1,0:T(8,128)(2,1)S(1)} %get-tuple-element.12), channel_id=1, source_target_pairs={{0,24},{4,28},{8,0},{12,4},{16,8},{20,12},{24,16},{28,20},{1,25},{... | collective-permute-start | bytes 393224 | tf_op jit(solution)/shard_map/ppermute | solution.py:417
  91.8 9.2 %collective-permute-start.10 = (bf16[2,512,128]{2,1,0:T(8,128)(2,1)S(1)}, bf16[2,512,128]{2,1,0:T(8,128)(2,1)S(1)}, u32[]{:S(2)}, u32[]{:S(2)}) collective-permute-start(bf16[2,512,128]{2,1,0:T(8,128)(2,1)S(1)} %collective-permute-done.4), channel_id=1, source_target_pairs={{0,4},{4,0},{8,12},{12,8},{16,20},{20,16},{24,28},{28,24},{1,5},{5... | collective-permute-start | bytes 786440 | tf_op jit(solution)/shard_map/ppermute | solution.py:420
  93.3 13.2 %collective-permute-start.11 = (bf16[2,512,128]{2,1,0:T(8,128)(2,1)S(1)}, bf16[2,512,128]{2,1,0:T(8,128)(2,1)S(1)}, u32[]{:S(2)}, u32[]{:S(2)}) collective-permute-start(bf16[2,512,128]{2,1,0:T(8,128)(2,1)S(1)} %collective-permute-done.6), channel_id=1, source_target_pairs={{0,4},{4,0},{8,12},{12,8},{16,20},{20,16},{24,28},{28,24},{1,5},{5... | collective-permute-start | bytes 786440 | tf_op jit(solution)/shard_map/ppermute | solution.py:420
  93.8 17.5 %collective-permute-start.12 = (bf16[2,512,128]{2,1,0:T(8,128)(2,1)S(1)}, bf16[2,512,128]{2,1,0:T(8,128)(2,1)S(1)}, u32[]{:S(2)}, u32[]{:S(2)}) collective-permute-start(bf16[2,512,128]{2,1,0:T(8,128)(2,1)S(1)} %collective-permute-done.8), channel_id=1, source_target_pairs={{0,4},{4,0},{8,12},{12,8},{16,20},{20,16},{24,28},{28,24},{1,5},{5... | collective-permute-start | bytes 786440 | tf_op jit(solution)/shard_map/ppermute | solution.py:420
  126.5 16.3 %collective-permute-start.13 = (bf16[512,128]{1,0:T(8,128)(2,1)S(1)}, bf16[512,128]{1,0:T(8,128)(2,1)S(1)}, u32[]{:S(2)}, u32[]{:S(2)}) collective-permute-start(bf16[512,128]{1,0:T(8,128)(2,1)S(1)} %get-tuple-element.21), channel_id=1, source_target_pairs={{0,24},{4,28},{8,0},{12,4},{16,8},{20,12},{24,16},{28,20},{1,25},{... | collective-permute-start | bytes 393224 | tf_op jit(solution)/shard_map/ppermute | solution.py:417
  130.6 12.4 %collective-permute-start.14 = (bf16[512,128]{1,0:T(8,128)(2,1)S(1)}, bf16[512,128]{1,0:T(8,128)(2,1)S(1)}, u32[]{:S(2)}, u32[]{:S(2)}) collective-permute-start(bf16[512,128]{1,0:T(8,128)(2,1)S(1)} %get-tuple-element.20), channel_id=1, source_target_pairs={{0,16},{4,20},{8,24},{12,28},{16,0},{20,4},{24,8},{28,12},{1,17},{... | collective-permute-start | bytes 393224 | tf_op jit(solution)/shard_map/ppermute | solution.py:417
  132.6 10.4 %collective-permute-start.15 = (bf16[512,128]{1,0:T(8,128)(2,1)S(1)}, bf16[512,128]{1,0:T(8,128)(2,1)S(1)}, u32[]{:S(2)}, u32[]{:S(2)}) collective-permute-start(bf16[512,128]{1,0:T(8,128)(2,1)S(1)} %get-tuple-element.19), channel_id=1, source_target_pairs={{0,8},{4,12},{8,16},{12,20},{16,24},{20,28},{24,0},{28,4},{1,9},{5... | collective-permute-start | bytes 393224 | tf_op jit(solution)/shard_map/ppermute | solution.py:417

commit v2 on v1

--- a/solution.py
+++ b/solution.py
@@ -163,15 +163,12 @@
     cosine,
     sine,
     prompt_mask,
-    query_w,
     key_w,
     value_w,
     down,
-    query_up,
     value_up,
     out,
     normed,
-    query_sum,
     key_sum,
     value_sum,
     down_sum,
@@ -194,22 +191,50 @@
             factor = lax.rsqrt(total / (len(blocks) * width) + EPS)
             for number, block in enumerate(blocks):
                 value = block[at, :].astype(jnp.float32)
-                normed[number, at, :] = (value * factor * gain[number]).astype(jnp.bfloat16)
+                normed[number, at, :] = (value * factor * gain[scalars[0] ^ number]).astype(jnp.bfloat16)
             return carry
 
         lax.fori_loop(0, rows // part, normalise, 0)
-        query_sum[...] = jnp.zeros_like(query_sum)
         key_sum[...] = jnp.zeros_like(key_sum)
         value_sum[...] = jnp.zeros_like(value_sum)
         down_sum[...] = jnp.zeros_like(down_sum)
 
     tile = normed[step]
-    query_sum[...] += jnp.dot(tile, query_w[...], preferred_element_type=jnp.float32)
     key_sum[...] += jnp.dot(tile, key_w[...], preferred_element_type=jnp.float32)
     value_sum[...] += jnp.dot(tile, value_w[...], preferred_element_type=jnp.float32)
     down_sum[...] += jnp.dot(tile, down[...], preferred_element_type=jnp.float32)
 
     @pl.when(step == len(blocks) - 1)
+    def _():
+        layer = scalars[1]
+        middle = (down_sum[...] * prompt_mask[...]).astype(jnp.bfloat16)
+        for head in range(LAYERS):
+            place = lax.rem(head - layer + LAYERS, LAYERS)
+            lanes = slice(head * HEAD, (head + 1) * HEAD)
+            key = key_sum[:, lanes]
+            value = value_sum[:, lanes] + ADAPTER_SCALE * jnp.dot(
+                middle, value_up[:, lanes], preferred_element_type=jnp.float32
+            )
+            turned = key * cosine[...] + pltpu.roll(key, HEAD // 2, 1) * sine[...]
+            out[place, 0] = turned.astype(jnp.bfloat16)
+            out[place, 1] = value.astype(jnp.bfloat16)
+
+
+def query_kernel(
+    scalars, normed, cosine, sine, prompt_mask, query_w, down, query_up, out, query_sum, down_sum
+):
+    step = pl.program_id(0)
+
+    @pl.when(step == 0)
+    def _():
+        query_sum[...] = jnp.zeros_like(query_sum)
+        down_sum[...] = jnp.zeros_like(down_sum)
+
+    tile = normed[0]
+    query_sum[...] += jnp.dot(tile, query_w[...], preferred_element_type=jnp.float32)
+    down_sum[...] += jnp.dot(tile, down[...], preferred_element_type=jnp.float32)
+
+    @pl.when(step == pl.num_programs(0) - 1)
     def _():
         layer = scalars[1]
         middle = (down_sum[...] * prompt_mask[...]).astype(jnp.bfloat16)
@@ -219,19 +244,13 @@
             query = query_sum[:, lanes] + ADAPTER_SCALE * jnp.dot(
                 middle, query_up[:, lanes], preferred_element_type=jnp.float32
             )
-            key = key_sum[:, lanes]
-            value = value_sum[:, lanes] + ADAPTER_SCALE * jnp.dot(
-                middle, value_up[:, lanes], preferred_element_type=jnp.float32
-            )
-            for slot, field in enumerate((query, key)):
-                turned = field * cosine[...] + pltpu.roll(field, HEAD // 2, 1) * sine[...]
-                out[place, slot] = turned.astype(jnp.bfloat16)
-            out[place, 2] = value.astype(jnp.bfloat16)
-
-
-def attend_kernel(scalars, mine, other, out, peak, total, summed):
+            turned = query * cosine[...] + pltpu.roll(query, HEAD // 2, 1) * sine[...]
+            out[place] = turned.astype(jnp.bfloat16)
+
+
+def attend_kernel(scalars, queries, mine, other, out, peak, total, summed):
     step = pl.program_id(0)
-    rows = mine.shape[2]
+    rows = queries.shape[1]
     layer, column = scalars[0], scalars[1]
     prompts = scalars.shape[0] - 2
     query_block = lax.rem(layer - step + LAYERS, LAYERS) * COLUMNS + column
@@ -245,7 +264,7 @@
         end = end + length
         first_start += jnp.where(end <= first, length, 0)
         last_start += jnp.where(end <= last, length, 0)
-    query = mine[step, 0]
+    query = queries[step]
     peak[...] = jnp.full_like(peak, MASKED)
     total[...] = jnp.zeros_like(total)
     summed[...] = jnp.zeros_like(summed)
@@ -291,7 +310,7 @@
                 @pl.when((same == is_mine) & (whole != masked))
                 def _():
                     if is_mine:
-                        visit(block, masked, mine[place, 1], mine[place, 2])
+                        visit(block, masked, mine[place, 0], mine[place, 1])
                     else:
                         visit(block, masked, other[place, 0], other[place, 1])
 
@@ -329,7 +348,6 @@
 
     across = flip(tokens, 2)
     near = flip(tokens, 1)
-    far = flip(across, 1)
 
     positions = req_index * row_count + jnp.arange(row_count, dtype=jnp.int32)
     starts, prompt = prompt_layout(lengths, positions)
@@ -361,8 +379,11 @@
     value_up = jnp.dot(
         pick_value.T, value_up_maps, preferred_element_type=jnp.float32
     ).astype(jnp.bfloat16)
-    order = tp_index ^ jnp.arange(peers, dtype=jnp.int32)
-    gain = input_norm_gain.reshape(peers, 1, width)[order]
+    gain = input_norm_gain.reshape(peers, 1, width)
+    across, gain, cosine, sine, prompt_mask, down, query_up, value_up = lax.optimization_barrier(
+        (across, gain, cosine, sine, prompt_mask, down, query_up, value_up)
+    )
+    far = flip(across, 1)
 
     def full(shape):
         return pl.BlockSpec(shape, lambda j, s: (0,) * len(shape))
@@ -370,7 +391,9 @@
     def weight(columns):
         return pl.BlockSpec((width, columns), lambda j, s: (s[0] ^ j, 0))
 
-    projected = pl.pallas_call(
+    places = jnp.stack([tp_index, layer]).astype(jnp.int32)
+    lanes = lane.shape[0]
+    key_value, normed = pl.pallas_call(
         project_kernel,
         grid_spec=pltpu.PrefetchScalarGridSpec(
             num_scalar_prefetch=1,
@@ -378,20 +401,24 @@
             in_specs=[full((row_count, width))] * 4
             + [full((peers, 1, width))]
             + [full((row_count, HEAD))] * 2
-            + [full((row_count, lane.shape[0]))]
-            + [weight(features)] * 3
-            + [weight(lane.shape[0])]
-            + [full((lane.shape[0], features))] * 2,
-            out_specs=full((LAYERS, 3, row_count, HEAD)),
-            scratch_shapes=[pltpu.VMEM((peers, row_count, width), jnp.bfloat16)]
-            + [pltpu.VMEM((row_count, features), jnp.float32)] * 3
-            + [pltpu.VMEM((row_count, lane.shape[0]), jnp.float32)],
+            + [full((row_count, lanes))]
+            + [weight(features)] * 2
+            + [weight(lanes), full((lanes, features))],
+            out_specs=[
+                full((LAYERS, 2, row_count, HEAD)),
+                full((peers, row_count, width)),
+            ],
+            scratch_shapes=[pltpu.VMEM((row_count, features), jnp.float32)] * 2
+            + [pltpu.VMEM((row_count, lanes), jnp.float32)],
         ),
-        out_shape=jax.ShapeDtypeStruct((LAYERS, 3, row_count, HEAD), jnp.bfloat16),
+        out_shape=[
+            jax.ShapeDtypeStruct((LAYERS, 2, row_count, HEAD), jnp.bfloat16),
+            jax.ShapeDtypeStruct((peers, row_count, width), jnp.bfloat16),
+        ],
         compiler_params=pltpu.CompilerParams(vmem_limit_bytes=48 * 1024 * 1024),
         name="project",
     )(
-        jnp.stack([tp_index, layer]).astype(jnp.int32),
+        places,
         tokens,
         near,
         across,
@@ -400,13 +427,35 @@
         cosine,
         sine,
         prompt_mask,
-        query_weight,
         key_weight,
         value_weight,
         down,
-        query_up,
         value_up,
     )
+    queries = pl.pallas_call(
+        query_kernel,
+        grid_spec=pltpu.PrefetchScalarGridSpec(
+            num_scalar_prefetch=1,
+            grid=(peers,),
+            in_specs=[pl.BlockSpec((1, row_count, width), lambda j, s: (j, 0, 0))]
+            + [full((row_count, HEAD))] * 2
+            + [full((row_count, lanes)), weight(features), weight(lanes)]
+            + [full((lanes, features))],
+            out_specs=full((LAYERS, row_count, HEAD)),
+            scratch_shapes=[
+                pltpu.VMEM((row_count, features), jnp.float32),
+                pltpu.VMEM((row_count, lanes), jnp.float32),
+            ],
+        ),
+        out_shape=jax.ShapeDtypeStruct((LAYERS, row_count, HEAD), jnp.bfloat16),
+        compiler_params=pltpu.CompilerParams(vmem_limit_bytes=48 * 1024 * 1024),
+        cost_estimate=pl.CostEstimate(
+            flops=2 * row_count * depth * (features + lanes),
+            bytes_accessed=2 * depth * (row_count + features),
+            transcendentals=0,
+        ),
+        name="project_queries",
+    )(places, normed, cosine, sine, prompt_mask, query_weight, down, query_up)
 
     def along(array, distance):
         pairs = [
@@ -419,22 +468,20 @@
     def swap(array):
         return lax.ppermute(array, "req", [(i, i ^ 1) for i in range(LAYERS * COLUMNS)])
 
-    mine = [projected[0]]
-    mine_kv = {s: along(projected[s, 1:], s) for s in (2, 1, 3)}
-    mine_q = {s: along(projected[s, :1], s) for s in (2, 1, 3)}
-    other = [swap(projected[0, 1:])] + [swap(mine_kv[s]) for s in range(1, LAYERS)]
-    mine = jnp.stack(
-        [projected[0]]
-        + [jnp.concatenate([mine_q[s], mine_kv[s]], axis=0) for s in range(1, LAYERS)]
-    )
-    other = jnp.stack(other)
+    arrived = {s: along(key_value[s], s) for s in (2, 1, 3)}
+    other = jnp.stack([swap(key_value[0])] + [swap(arrived[s]) for s in range(1, LAYERS)])
+    mine = jnp.stack([key_value[0]] + [arrived[s] for s in range(1, LAYERS)])
+    queries = jnp.stack(
+        [queries[0]] + [along(queries[s], s) for s in range(1, LAYERS)]
+    )
     attended = pl.pallas_call(
         attend_kernel,
         grid_spec=pltpu.PrefetchScalarGridSpec(
             num_scalar_prefetch=1,
             grid=(LAYERS,),
             in_specs=[
-                full((LAYERS, 3, row_count, HEAD)),
+                full((LAYERS, row_count, HEAD)),
+                full((LAYERS, 2, row_count, HEAD)),
                 full((LAYERS, 2, row_count, HEAD)),
             ],
             out_specs=pl.BlockSpec((1, row_count, HEAD), lambda j, s: (j, 0, 0)),
@@ -449,6 +496,7 @@
         name="attend",
     )(
         jnp.concatenate([jnp.stack([layer, column]).astype(jnp.int32), lengths]),
+        queries,
         mine,
         other,
     )

time: 146 us -> 138 us (0.945); the launches traced: 144 us -> 138 us
  waiting for transfers between devices: 62.2 us -> 52.1 us
  Pallas kernels: 31.7 us -> 39.9 us
  local copies, waits for them, and re-layouts: 6.13 us -> 1.84 us
    ppermute x9, waiting for transfers between devices: 27.8 us -> 20 us  [along(): return lax.ppermute(array, 'req', pairs)]
    pallas_call x0 -> x1, Pallas kernels: none -> 7.35 us  [fast_body(): pl.pallas_call(query_kernel, grid_spec=pltpu.PrefetchScalarGridSpec(num_s...]
    ppermute x3, waiting for transfers between devices: 18.8 us -> 14.1 us  [flip(): return lax.ppermute(array, 'tp', [(i, i ^ bit) for i in range(peers)])]
    gather x2 -> x0, local copies, waits for them, and re-layouts: 2.62 us -> none  [fast_body(): gain = input_norm_gain.reshape(peers, 1, width)[order]]
    pallas_call x1, Pallas kernels: 15.1 us -> 17.7 us  [fast_body(): pl.pallas_call(attend_kernel, grid_spec=pltpu.PrefetchScalarGridSpec(num_...]
    ppermute x4, waiting for transfers between devices: 15.6 us -> 18 us  [swap(): lax.ppermute(array, 'req', [(i, i ^ 1) for i in range(LAYERS * COLUMNS)])]
    pallas_call x1, Pallas kernels: 16.6 us -> 14.9 us  [fast_body(): pl.pallas_call(project_kernel, grid_spec=pltpu.PrefetchScalarGridSpec(num...]
  transfers between devices with their start and end apart: 16 -> 16, of which waited for: 7 -> 9; matrix products, arithmetic and copies ran while one was open for 12% -> 9% of each run, Pallas kernels for 0% -> 5%
where the time goes in v2:
time: 138 us
  waiting for transfers between devices  52.1 us (38%)
  Pallas kernels  39.9 us (29%)
  starting transfers between devices  23 us (17%)
  matrix products  8.13 us (6%)
  between operations  7.78 us (6%)
  other arithmetic  5.1 us (4%)
  local copies, waits for them, and re-layouts  1.84 us (1%)
    ppermute x9, waiting for transfers between devices, along(): return lax.ppermute(array, 'req', pairs)  20 us
    ppermute x4, waiting for transfers between devices, swap(): lax.ppermute(array, 'req', [(i, i ^ 1) for i in range(LAYERS * COLUMNS)])  18 us
    pallas_call x1, Pallas kernels, fast_body(): pl.pallas_call(attend_kernel, grid_spec=pltpu.PrefetchScalarGridSpec(num_...  17.7 us
    ppermute x9, starting transfers between devices, along(): return lax.ppermute(array, 'req', pairs)  16 us
    pallas_call x1, Pallas kernels, fast_body(): pl.pallas_call(project_kernel, grid_spec=pltpu.PrefetchScalarGridSpec(num...  14.9 us
    ppermute x3, waiting for transfers between devices, flip(): return lax.ppermute(array, 'tp', [(i, i ^ bit) for i in range(peers)])  14.1 us
    pallas_call x1, Pallas kernels, fast_body(): pl.pallas_call(query_kernel, grid_spec=pltpu.PrefetchScalarGridSpec(num_s...  7.35 us
    ppermute x4, starting transfers between devices, swap(): lax.ppermute(array, 'req', [(i, i ^ 1) for i in range(LAYERS * COLUMNS)])  4.06 us
  transfers between devices with their start and end apart: 16, of which 9 were waited for; matrix products, arithmetic and copies ran while one was open for 9% of the time, Pallas kernels for 5%

profile of v2, /device:TPU:0, one launch (start us, length us, event | category | flops | bytes accessed | tf_op | source)
XLA Modules:
  0.0 137.9 jit_solution(17624161359676725662)
XLA Ops:
  0.0 2.9 %collective-permute-start.1 = (bf16[512,1024]{1,0:T(8,128)(2,1)}, bf16[512,1024]{1,0:T(8,128)(2,1)S(1)}, u32[]{:S(2)}, u32[]{:S(2)}) collective-permute-start(bf16[512,1024]{1,0:T(8,128)(2,1)} %own.1), channel_id=1, source_target_pairs={{0,2},{1,3},{2,0},{3,1},{4,6},{5,7},{6,4},{7,5},{8,10},{9,11},{10,... | collective-permute-start | bytes 3145736 | tf_op jit(solution)/shard_map/ppermute | solution.py:347
  3.0 0.8 reduce-window.8
  3.8 0.7 fusion.19
  5.5 1.0 fusion.17
  6.7 0.9 convolution_convert_fusion.value_up
  7.7 1.4 %convolution_convert_fusion.1.query_up = bf16[128,512]{1,0:T(8,128)(2,1)S(1)} fusion(bf16[512,512]{1,0:T(8,128)(2,1)} %param.18, s32[128]{0:T(128)S(1)} %fusion.20, pred[128]{0:T(512)(128)(4,1)S(1)} %iota_compare_fusion.2), kind=kOutput, calls=%fused_computation.4 | convolution fusion | flops 67305472 | bytes 656000 | tf_op jit(solution)/shard_map/dot_general | solution.py:376
  9.1 3.5 %fusion.5 = f32[128,4096]{0,1:T(8,128)S(1)} fusion(bf16[4096,512]{1,0:T(8,128)(2,1)} %param.16, s32[128]{0:T(128)S(1)} %fusion.20, pred[128]{0:T(512)(128)(4,1)S(1)} %iota_compare_fusion.2), kind=kOutput, calls=%fused_computation.20 | convolution fusion | flops 537001984 | bytes 6292096 | tf_op jit(solution)/shard_map/dot_general | solution.py:373
  12.6 2.3 %fusion.1.down = bf16[4096,128]{1,0:T(8,128)(2,1)} fusion(f32[128,4096]{0,1:T(8,128)S(1)} %fusion.5, bf16[4096,512]{1,0:T(8,128)(2,1)S(1)} %copy-done.5, s32[128]{0:T(128)S(1)} %fusion.20, pred[128]{0:T(512)(128)(4,1)S(1)} %copy-done.7), kind=kOutput, calls=%fused_computation.2 | convolution fusion | flops 538050560 | bytes 7340672 | tf_op jit(solution)/shard_map/dot_general | solution.py:374
  14.9 11.4 %collective-permute-done.1.across = bf16[512,1024]{1,0:T(8,128)(2,1)S(1)} collective-permute-done((bf16[512,1024]{1,0:T(8,128)(2,1)}, bf16[512,1024]{1,0:T(8,128)(2,1)S(1)}, u32[]{:S(2)}, u32[]{:S(2)}) %collective-permute-start.1) | collective-permute-done | bytes 1048608 | tf_op jit(solution)/shard_map/ppermute | solution.py:347
  26.4 2.7 %collective-permute-done.2.far = bf16[512,1024]{1,0:T(8,128)(2,1)} collective-permute-done((bf16[512,1024]{1,0:T(8,128)(2,1)S(1)}, bf16[512,1024]{1,0:T(8,128)(2,1)}, u32[]{:S(2)}, u32[]{:S(2)}) %collective-permute-start.2) | collective-permute-done | bytes 1048608 | tf_op jit(solution)/shard_map/ppermute | solution.py:347
  29.1 0.9 copy-done.3
  30.0 14.9 %project.1 = (bf16[4,2,512,128]{3,2,1,0:T(8,128)(2,1)S(1)}, bf16[4,512,1024]{2,1,0:T(8,128)(2,1)}) custom-call(s32[2]{0:T(128)S(1)} %pad_add_fusion.1.scalars, bf16[512,1024]{1,0:T(8,128)(2,1)S(1)} %copy-done.2, bf16[512,1024]{1,0:T(8,128)(2,1)} %collective-permute-done.near, bf16[512,1024]{1,0:T(8,128)(2,1)S(1)} %collective-permute-done.1.across, ...), custom_call_target="tpu_custom_call" | custom-call | tf_op jit(solution)/shard_map/project/pallas_call | solution.py:396
  45.0 1.9 %collective-permute-start.6 = (bf16[2,512,128]{2,1,0:T(8,128)(2,1)S(1)}, bf16[2,512,128]{2,1,0:T(8,128)(2,1)S(1)}, u32[]{:S(2)}, u32[]{:S(2)}) collective-permute-start(bf16[2,512,128]{2,1,0:T(8,128)(2,1)S(1)} %get-tuple-element.30), channel_id=1, source_target_pairs={{0,8},{4,12},{8,16},{12,20},{16,24},{20,28},{24,0},{28,4},{1,9},{5... | collective-permute-start | bytes 786440 | tf_op jit(solution)/shard_map/ppermute | solution.py:466
  46.9 2.6 %collective-permute-start.7 = (bf16[2,512,128]{2,1,0:T(8,128)(2,1)S(1)}, bf16[2,512,128]{2,1,0:T(8,128)(2,1)S(1)}, u32[]{:S(2)}, u32[]{:S(2)}) collective-permute-start(bf16[2,512,128]{2,1,0:T(8,128)(2,1)S(1)} %get-tuple-element.29), channel_id=1, source_target_pairs={{0,16},{4,20},{8,24},{12,28},{16,0},{20,4},{24,8},{28,12},{1,17},{... | collective-permute-start | bytes 786440 | tf_op jit(solution)/shard_map/ppermute | solution.py:466
  49.5 1.4 collective-permute-start.8
  50.8 7.4 %project_queries.1 = bf16[4,512,128]{2,1,0:T(8,128)(2,1)S(1)} custom-call(s32[2]{0:T(128)S(1)} %pad_add_fusion.1.scalars, bf16[4,512,1024]{2,1,0:T(8,128)(2,1)} %get-tuple-element.22.normed, f32[512,128]{1,0:T(8,128)S(1)} %get-tuple-element.17.cosine, f32[512,128]{1,0:T(8,128)S(1)} %get-tuple-element.18.sine, ...), custom_call_target="tpu_custom_call" | custom-call | flops 2684354560 | bytes 8388608 | tf_op jit(solution)/shard_map/project_queries/pallas_call | solution.py:435
  58.5 2.8 %collective-permute-start.5 = (bf16[512,128]{1,0:T(8,128)(2,1)S(1)}, bf16[512,128]{1,0:T(8,128)(2,1)S(1)}, u32[]{:S(2)}, u32[]{:S(2)}) collective-permute-start(bf16[512,128]{1,0:T(8,128)(2,1)S(1)} %get-tuple-element.41), channel_id=1, source_target_pairs={{0,24},{4,28},{8,0},{12,4},{16,8},{20,12},{24,16},{28,20},{1,25},{... | collective-permute-start | bytes 393224 | tf_op jit(solution)/shard_map/ppermute | solution.py:466
  61.3 16.8 %collective-permute-done.4 = bf16[512,128]{1,0:T(8,128)(2,1)S(1)} collective-permute-done((bf16[512,128]{1,0:T(8,128)(2,1)S(1)}, bf16[512,128]{1,0:T(8,128)(2,1)S(1)}, u32[]{:S(2)}, u32[]{:S(2)}) %collective-permute-start.4) | collective-permute-done | bytes 131104 | tf_op jit(solution)/shard_map/ppermute | solution.py:466
  78.2 1.7 %collective-permute-start.3 = (bf16[512,128]{1,0:T(8,128)(2,1)S(1)}, bf16[512,128]{1,0:T(8,128)(2,1)S(1)}, u32[]{:S(2)}, u32[]{:S(2)}) collective-permute-start(bf16[512,128]{1,0:T(8,128)(2,1)S(1)} %get-tuple-element.43), channel_id=1, source_target_pairs={{0,8},{4,12},{8,16},{12,20},{16,24},{20,28},{24,0},{28,4},{1,9},{5... | collective-permute-start | bytes 393224 | tf_op jit(solution)/shard_map/ppermute | solution.py:466
  79.9 1.5 %collective-permute-start.9 = (bf16[2,512,128]{2,1,0:T(8,128)(2,1)S(1)}, bf16[2,512,128]{2,1,0:T(8,128)(2,1)S(1)}, u32[]{:S(2)}, u32[]{:S(2)}) collective-permute-start(bf16[2,512,128]{2,1,0:T(8,128)(2,1)S(1)} %get-tuple-element.27), channel_id=1, source_target_pairs={{0,4},{4,0},{8,12},{12,8},{16,20},{20,16},{24,28},{28,24},{1,5},{5... | collective-permute-start | bytes 786440 | tf_op jit(solution)/shard_map/ppermute | solution.py:469
  82.0 1.5 %collective-permute-start.11 = (bf16[2,512,128]{2,1,0:T(8,128)(2,1)S(1)}, bf16[2,512,128]{2,1,0:T(8,128)(2,1)S(1)}, u32[]{:S(2)}, u32[]{:S(2)}) collective-permute-start(bf16[2,512,128]{2,1,0:T(8,128)(2,1)S(1)} %collective-permute-done.7), channel_id=1, source_target_pairs={{0,4},{4,0},{8,12},{12,8},{16,20},{20,16},{24,28},{28,24},{1,5},{5... | collective-permute-start | bytes 786440 | tf_op jit(solution)/shard_map/ppermute | solution.py:469
  84.0 1.6 %collective-permute-done.3 = bf16[512,128]{1,0:T(8,128)(2,1)S(1)} collective-permute-done((bf16[512,128]{1,0:T(8,128)(2,1)S(1)}, bf16[512,128]{1,0:T(8,128)(2,1)S(1)}, u32[]{:S(2)}, u32[]{:S(2)}) %collective-permute-start.3) | collective-permute-done | bytes 131104 | tf_op jit(solution)/shard_map/ppermute | solution.py:466
  85.8 3.4 %collective-permute-done.9 = bf16[2,512,128]{2,1,0:T(8,128)(2,1)S(1)} collective-permute-done((bf16[2,512,128]{2,1,0:T(8,128)(2,1)S(1)}, bf16[2,512,128]{2,1,0:T(8,128)(2,1)S(1)}, u32[]{:S(2)}, u32[]{:S(2)}) %collective-permute-start.9) | collective-permute-done | bytes 262176 | tf_op jit(solution)/shard_map/ppermute | solution.py:469
  89.2 5.6 %collective-permute-done.10 = bf16[2,512,128]{2,1,0:T(8,128)(2,1)S(1)} collective-permute-done((bf16[2,512,128]{2,1,0:T(8,128)(2,1)S(1)}, bf16[2,512,128]{2,1,0:T(8,128)(2,1)S(1)}, u32[]{:S(2)}, u32[]{:S(2)}) %collective-permute-start.10) | collective-permute-done | bytes 262176 | tf_op jit(solution)/shard_map/ppermute | solution.py:469
  94.8 5.6 %collective-permute-done.11 = bf16[2,512,128]{2,1,0:T(8,128)(2,1)S(1)} collective-permute-done((bf16[2,512,128]{2,1,0:T(8,128)(2,1)S(1)}, bf16[2,512,128]{2,1,0:T(8,128)(2,1)S(1)}, u32[]{:S(2)}, u32[]{:S(2)}) %collective-permute-start.11) | collective-permute-done | bytes 262176 | tf_op jit(solution)/shard_map/ppermute | solution.py:469
  100.4 3.4 %collective-permute-done.12 = bf16[2,512,128]{2,1,0:T(8,128)(2,1)S(1)} collective-permute-done((bf16[2,512,128]{2,1,0:T(8,128)(2,1)S(1)}, bf16[2,512,128]{2,1,0:T(8,128)(2,1)S(1)}, u32[]{:S(2)}, u32[]{:S(2)}) %collective-permute-start.12) | collective-permute-done | bytes 262176 | tf_op jit(solution)/shard_map/ppermute | solution.py:469
  103.9 17.7 %attend.1 = bf16[4,512,128]{2,1,0:T(8,128)(2,1)S(1)} custom-call(s32[6]{0:T(128)S(1)} %pad_add_fusion.scalars, bf16[4,512,128]{2,1,0:T(8,128)(2,1)S(1)} %pad_maximum_fusion.2.queries, bf16[4,2,512,128]{3,2,1,0:T(8,128)(2,1)S(1)} %pad_maximum_fusion.mine, bf16[4,2,512,128]{3,2,1,0:T(8,128)(2,1)S(1)} %pad_maximum_fusion.1.other), custom_call_target="tpu_custom_call" | custom-call | tf_op jit(solution)/shard_map/attend/pallas_call | solution.py:477
  121.7 3.2 %collective-permute-start.13 = (bf16[512,128]{1,0:T(8,128)(2,1)S(1)}, bf16[512,128]{1,0:T(8,128)(2,1)S(1)}, u32[]{:S(2)}, u32[]{:S(2)}) collective-permute-start(bf16[512,128]{1,0:T(8,128)(2,1)S(1)} %get-tuple-element.39), channel_id=1, source_target_pairs={{0,24},{4,28},{8,0},{12,4},{16,8},{20,12},{24,16},{28,20},{1,25},{... | collective-permute-start | bytes 393224 | tf_op jit(solution)/shard_map/ppermute | solution.py:466
  124.8 1.1 collective-permute-start.14
  125.9 1.2 collective-permute-start.15
  135.4 1.5 %collective-permute-done.14 = bf16[512,128]{1,0:T(8,128)(2,1)S(1)} collective-permute-done((bf16[512,128]{1,0:T(8,128)(2,1)S(1)}, bf16[512,128]{1,0:T(8,128)(2,1)S(1)}, u32[]{:S(2)}, u32[]{:S(2)}) %collective-permute-start.14) | collective-permute-done | bytes 131104 | tf_op jit(solution)/shard_map/ppermute | solution.py:466
  137.0 0.9 pad_maximum_fusion.4
  (51 shorter events, 3.9 us)
Async XLA Ops:
  0.0 6.7 %copy-start = (bf16[512,512]{1,0:T(8,128)(2,1)S(1)}, bf16[512,512]{1,0:T(8,128)(2,1)}, u32[]{:S(2)}) copy-start(bf16[512,512]{1,0:T(8,128)(2,1)} %param.19) | copy-start | bytes 1572868
  0.0 26.3 %collective-permute-start.1 = (bf16[512,1024]{1,0:T(8,128)(2,1)}, bf16[512,1024]{1,0:T(8,128)(2,1)S(1)}, u32[]{:S(2)}, u32[]{:S(2)}) collective-permute-start(bf16[512,1024]{1,0:T(8,128)(2,1)} %own.1), channel_id=1, source_target_pairs={{0,2},{1,3},{2,0},{3,1},{4,6},{5,7},{6,4},{7,5},{8,10},{9,11},{10,... | collective-permute-start | bytes 3145736 | tf_op jit(solution)/shard_map/ppermute | solution.py:347
  2.9 23.4 %collective-permute-start = (bf16[512,1024]{1,0:T(8,128)(2,1)}, bf16[512,1024]{1,0:T(8,128)(2,1)}, u32[]{:S(2)}, u32[]{:S(2)}) collective-permute-start(bf16[512,1024]{1,0:T(8,128)(2,1)} %own.1), channel_id=1, source_target_pairs={{0,1},{1,0},{2,3},{3,2},{4,5},{5,4},{6,7},{7,6},{8,9},{9,8},{10,11... | collective-permute-start | bytes 3145736 | tf_op jit(solution)/shard_map/ppermute | solution.py:347
  3.0 4.7 %copy-start.6 = (pred[128]{0:T(512)(128)(4,1)}, pred[128]{0:T(512)(128)(4,1)S(1)}, u32[]{:S(2)}) copy-start(pred[128]{0:T(512)(128)(4,1)S(1)} %fusion.23) | copy-start | bytes 388
  6.5 6.1 %copy-start.5 = (bf16[4096,512]{1,0:T(8,128)(2,1)S(1)}, bf16[4096,512]{1,0:T(8,128)(2,1)}, u32[]{:S(2)}) copy-start(bf16[4096,512]{1,0:T(8,128)(2,1)} %param.17) | copy-start | bytes 12582916
  7.7 4.9 %copy-start.7 = (pred[128]{0:T(512)(128)(4,1)S(1)}, pred[128]{0:T(512)(128)(4,1)}, u32[]{:S(2)}) copy-start(pred[128]{0:T(512)(128)(4,1)} %copy-done.6) | copy-start | bytes 388
  12.6 16.5 %copy-start.2 = (bf16[512,1024]{1,0:T(8,128)(2,1)S(1)}, bf16[512,1024]{1,0:T(8,128)(2,1)}, u32[]{:S(2)}) copy-start(bf16[512,1024]{1,0:T(8,128)(2,1)} %own.1) | copy-start | bytes 3145732
  12.6 16.5 %copy-start.4 = (f32[4096]{0:T(1024)S(1)}, f32[4096]{0:T(1024)}, u32[]{:S(2)}) copy-start(f32[4096]{0:T(1024)} %param.12) | copy-start | bytes 49156
  26.3 2.8 %collective-permute-start.2 = (bf16[512,1024]{1,0:T(8,128)(2,1)S(1)}, bf16[512,1024]{1,0:T(8,128)(2,1)}, u32[]{:S(2)}, u32[]{:S(2)}) collective-permute-start(bf16[512,1024]{1,0:T(8,128)(2,1)S(1)} %collective-permute-done.1.across), channel_id=1, source_target_pairs={{0,1},{1,0},{2,3},{3,2},{4,5},{5,4},{6,7},{7,6},{8,9},{9,8},{10,11... | collective-permute-start | bytes 3145736 | tf_op jit(solution)/shard_map/ppermute | solution.py:347
  26.4 24.4 %copy-start.1 = (bf16[4096,128]{1,0:T(8,128)(2,1)S(1)}, bf16[4096,128]{1,0:T(8,128)(2,1)}, u32[]{:S(2)}) copy-start(bf16[4096,128]{1,0:T(8,128)(2,1)} %fusion.1.down) | copy-start | bytes 3145732
  29.1 0.9 copy-start.3
  45.0 36.5 %collective-permute-start.6 = (bf16[2,512,128]{2,1,0:T(8,128)(2,1)S(1)}, bf16[2,512,128]{2,1,0:T(8,128)(2,1)S(1)}, u32[]{:S(2)}, u32[]{:S(2)}) collective-permute-start(bf16[2,512,128]{2,1,0:T(8,128)(2,1)S(1)} %get-tuple-element.30), channel_id=1, source_target_pairs={{0,8},{4,12},{8,16},{12,20},{16,24},{20,28},{24,0},{28,4},{1,9},{5... | collective-permute-start | bytes 786440 | tf_op jit(solution)/shard_map/ppermute | solution.py:466
  46.9 35.1 %collective-permute-start.7 = (bf16[2,512,128]{2,1,0:T(8,128)(2,1)S(1)}, bf16[2,512,128]{2,1,0:T(8,128)(2,1)S(1)}, u32[]{:S(2)}, u32[]{:S(2)}) collective-permute-start(bf16[2,512,128]{2,1,0:T(8,128)(2,1)S(1)} %get-tuple-element.29), channel_id=1, source_target_pairs={{0,16},{4,20},{8,24},{12,28},{16,0},{20,4},{24,8},{28,12},{1,17},{... | collective-permute-start | bytes 786440 | tf_op jit(solution)/shard_map/ppermute | solution.py:466
  49.5 34.0 %collective-permute-start.8 = (bf16[2,512,128]{2,1,0:T(8,128)(2,1)S(1)}, bf16[2,512,128]{2,1,0:T(8,128)(2,1)S(1)}, u32[]{:S(2)}, u32[]{:S(2)}) collective-permute-start(bf16[2,512,128]{2,1,0:T(8,128)(2,1)S(1)} %get-tuple-element.28), channel_id=1, source_target_pairs={{0,24},{4,28},{8,0},{12,4},{16,8},{20,12},{24,16},{28,20},{1,25},{... | collective-permute-start | bytes 786440 | tf_op jit(solution)/shard_map/ppermute | solution.py:466
  50.8 29.0 %copy-start.8 = (s32[4]{0:T(128)S(1)}, s32[4]{0:T(128)}, u32[]{:S(2)}) copy-start(s32[4]{0:T(128)} %param.20) | copy-start | bytes 52
  58.2 19.9 %collective-permute-start.4 = (bf16[512,128]{1,0:T(8,128)(2,1)S(1)}, bf16[512,128]{1,0:T(8,128)(2,1)S(1)}, u32[]{:S(2)}, u32[]{:S(2)}) collective-permute-start(bf16[512,128]{1,0:T(8,128)(2,1)S(1)} %get-tuple-element.42), channel_id=1, source_target_pairs={{0,16},{4,20},{8,24},{12,28},{16,0},{20,4},{24,8},{28,12},{1,17},{... | collective-permute-start | bytes 393224 | tf_op jit(solution)/shard_map/ppermute | solution.py:466
  58.5 21.4 %collective-permute-start.5 = (bf16[512,128]{1,0:T(8,128)(2,1)S(1)}, bf16[512,128]{1,0:T(8,128)(2,1)S(1)}, u32[]{:S(2)}, u32[]{:S(2)}) collective-permute-start(bf16[512,128]{1,0:T(8,128)(2,1)S(1)} %get-tuple-element.41), channel_id=1, source_target_pairs={{0,24},{4,28},{8,0},{12,4},{16,8},{20,12},{24,16},{28,20},{1,25},{... | collective-permute-start | bytes 393224 | tf_op jit(solution)/shard_map/ppermute | solution.py:466
  78.2 7.4 %collective-permute-start.3 = (bf16[512,128]{1,0:T(8,128)(2,1)S(1)}, bf16[512,128]{1,0:T(8,128)(2,1)S(1)}, u32[]{:S(2)}, u32[]{:S(2)}) collective-permute-start(bf16[512,128]{1,0:T(8,128)(2,1)S(1)} %get-tuple-element.43), channel_id=1, source_target_pairs={{0,8},{4,12},{8,16},{12,20},{16,24},{20,28},{24,0},{28,4},{1,9},{5... | collective-permute-start | bytes 393224 | tf_op jit(solution)/shard_map/ppermute | solution.py:466
  79.9 9.3 %collective-permute-start.9 = (bf16[2,512,128]{2,1,0:T(8,128)(2,1)S(1)}, bf16[2,512,128]{2,1,0:T(8,128)(2,1)S(1)}, u32[]{:S(2)}, u32[]{:S(2)}) collective-permute-start(bf16[2,512,128]{2,1,0:T(8,128)(2,1)S(1)} %get-tuple-element.27), channel_id=1, source_target_pairs={{0,4},{4,0},{8,12},{12,8},{16,20},{20,16},{24,28},{28,24},{1,5},{5... | collective-permute-start | bytes 786440 | tf_op jit(solution)/shard_map/ppermute | solution.py:469
  81.5 13.3 %collective-permute-start.10 = (bf16[2,512,128]{2,1,0:T(8,128)(2,1)S(1)}, bf16[2,512,128]{2,1,0:T(8,128)(2,1)S(1)}, u32[]{:S(2)}, u32[]{:S(2)}) collective-permute-start(bf16[2,512,128]{2,1,0:T(8,128)(2,1)S(1)} %collective-permute-done.6), channel_id=1, source_target_pairs={{0,4},{4,0},{8,12},{12,8},{16,20},{20,16},{24,28},{28,24},{1,5},{5... | collective-permute-start | bytes 786440 | tf_op jit(solution)/shard_map/ppermute | solution.py:469
  82.0 18.4 %collective-permute-start.11 = (bf16[2,512,128]{2,1,0:T(8,128)(2,1)S(1)}, bf16[2,512,128]{2,1,0:T(8,128)(2,1)S(1)}, u32[]{:S(2)}, u32[]{:S(2)}) collective-permute-start(bf16[2,512,128]{2,1,0:T(8,128)(2,1)S(1)} %collective-permute-done.7), channel_id=1, source_target_pairs={{0,4},{4,0},{8,12},{12,8},{16,20},{20,16},{24,28},{28,24},{1,5},{5... | collective-permute-start | bytes 786440 | tf_op jit(solution)/shard_map/ppermute | solution.py:469
  83.5 20.3 %collective-permute-start.12 = (bf16[2,512,128]{2,1,0:T(8,128)(2,1)S(1)}, bf16[2,512,128]{2,1,0:T(8,128)(2,1)S(1)}, u32[]{:S(2)}, u32[]{:S(2)}) collective-permute-start(bf16[2,512,128]{2,1,0:T(8,128)(2,1)S(1)} %collective-permute-done.8), channel_id=1, source_target_pairs={{0,4},{4,0},{8,12},{12,8},{16,20},{20,16},{24,28},{28,24},{1,5},{5... | collective-permute-start | bytes 786440 | tf_op jit(solution)/shard_map/ppermute | solution.py:469
  121.7 13.7 %collective-permute-start.13 = (bf16[512,128]{1,0:T(8,128)(2,1)S(1)}, bf16[512,128]{1,0:T(8,128)(2,1)S(1)}, u32[]{:S(2)}, u32[]{:S(2)}) collective-permute-start(bf16[512,128]{1,0:T(8,128)(2,1)S(1)} %get-tuple-element.39), channel_id=1, source_target_pairs={{0,24},{4,28},{8,0},{12,4},{16,8},{20,12},{24,16},{28,20},{1,25},{... | collective-permute-start | bytes 393224 | tf_op jit(solution)/shard_map/ppermute | solution.py:466
  124.8 12.1 %collective-permute-start.14 = (bf16[512,128]{1,0:T(8,128)(2,1)S(1)}, bf16[512,128]{1,0:T(8,128)(2,1)S(1)}, u32[]{:S(2)}, u32[]{:S(2)}) collective-permute-start(bf16[512,128]{1,0:T(8,128)(2,1)S(1)} %get-tuple-element.38), channel_id=1, source_target_pairs={{0,16},{4,20},{8,24},{12,28},{16,0},{20,4},{24,8},{28,12},{1,17},{... | collective-permute-start | bytes 393224 | tf_op jit(solution)/shard_map/ppermute | solution.py:466
  125.9 11.0 %collective-permute-start.15 = (bf16[512,128]{1,0:T(8,128)(2,1)S(1)}, bf16[512,128]{1,0:T(8,128)(2,1)S(1)}, u32[]{:S(2)}, u32[]{:S(2)}) collective-permute-start(bf16[512,128]{1,0:T(8,128)(2,1)S(1)} %get-tuple-element.37), channel_id=1, source_target_pairs={{0,8},{4,12},{8,16},{12,20},{16,24},{20,28},{24,0},{28,4},{1,9},{5... | collective-permute-start | bytes 393224 | tf_op jit(solution)/shard_map/ppermute | solution.py:466
